TPU v7x, 32 devices: a whole 2x2x4 slice. The times are simulated.
32 devices in a mesh: dp: 4 (over z), ctx: 4 (over y, x), tensor: 2 (over core).
Axes of the slice: x: 2, y: 2, z: 4, core: 2. Of those that a mesh axis runs over, the one named last changes fastest.
Arguments:
- hidden: bfloat16 [8, 2048, 1024], P('dp', 'ctx'), may hold values from -6 to 6
- out_grad: bfloat16 [8, 2048, 1024], P('dp', 'ctx'), may hold values from -6 to 6
- pre_gain: float32 [2, 1024], replicated, may hold values from 0.5 to 1.5
- gate_inner_weight: bfloat16 [2, 1024, 2, 2048], P(None, 'ctx', None, 'tensor'), may hold values from -0.1875 to 0.1875
- state_maps_weight: bfloat16 [2, 1024, 256], P(None, 'ctx', 'tensor'), may hold values from -0.1875 to 0.1875
- step_size_weight: bfloat16 [2, 1024, 32], P(None, 'ctx', 'tensor'), may hold values from -0.1875 to 0.1875
- conv_x: float32 [2, 4, 2048], P(None, None, 'tensor'), may hold values from -3 to 3
- bias_x: float32 [2, 2048], P(None, 'tensor'), may hold values from -3 to 3
- conv_bc: float32 [2, 4, 256], P(None, None, 'tensor'), may hold values from -3 to 3
- bias_bc: float32 [2, 256], P(None, 'tensor'), may hold values from -3 to 3
- dt_bias: float32 [2, 32], P(None, 'tensor'), may hold values from -7 to -2
- a_log: float32 [2, 32], P(None, 'tensor'), may hold values from 0 to 2.77
- d_skip: float32 [2, 32], P(None, 'tensor'), may hold values from 0.1 to 1.9
- norm_gain: float32 [2, 2048], P(None, 'tensor'), may hold values from 0.5 to 1.5
- output_weight: bfloat16 [2, 2048, 1024], P(None, 'tensor', 'ctx'), may hold values from -0.125 to 0.125
Outputs:
- output: float32 [8, 2048, 1024], P('dp', 'ctx')
- grad_hidden: float32 [8, 2048, 1024], P('dp', 'ctx')
- grad_pre_gain: float32 [2, 1024], replicated
- grad_proj_zx: float32 [2, 1024, 2, 2048], P(None, 'ctx', None, 'tensor')
- grad_proj_bc: float32 [2, 1024, 256], P(None, 'ctx', 'tensor')
- grad_proj_dt: float32 [2, 1024, 32], P(None, 'ctx', 'tensor')
- grad_conv_x: float32 [2, 4, 2048], P(None, None, 'tensor')
- grad_bias_x: float32 [2, 2048], P(None, 'tensor')
- grad_conv_bc: float32 [2, 4, 256], P(None, None, 'tensor')
- grad_bias_bc: float32 [2, 256], P(None, 'tensor')
- grad_dt_bias: float32 [2, 32], P(None, 'tensor')
- grad_a_log: float32 [2, 32], P(None, 'tensor')
- grad_d_skip: float32 [2, 32], P(None, 'tensor')
- grad_norm_gain: float32 [2, 2048], P(None, 'tensor')
- grad_proj_out: float32 [2, 2048, 1024], P(None, 'tensor', 'ctx')
All inputs are finite; a program needn't handle non-finite values.
Results may differ from a plain program's by a relative error of at most 0.03.
Values may be sent and summed in bfloat16 or wider, within the bound.
A program may use at most 256 MiB of HBM per device.

v0:
```python
import jax
import jax.numpy as jnp
from jax import lax
from jax.sharding import PartitionSpec as P

HEAD_DIM = 64
STATE = 128
KCONV = 4
GROUP = 256
LAYERS = 2
DI = 2048


epsilon = 1e-05
highest_precision = lax.Precision.HIGHEST


def passed_along(shard, axis, by):
    count = lax.axis_size(axis)
    pairs = [(i, i + by) for i in range(count) if 0 <= i + by < count]
    return lax.ppermute(shard, axis, pairs)


def prefix(shard, axis, combine, identity):
    count, place = (lax.axis_size(axis), lax.axis_index(axis))
    everything = jax.tree.map(
        lambda part, kind: lax.all_gather(part.astype(kind), axis),
        shard,
        (jnp.bfloat16, jnp.bfloat16),
    )
    start = jax.tree.map(
        lambda part, zero: jnp.broadcast_to(jnp.asarray(zero, part.dtype), part.shape),
        shard,
        identity,
    )

    def hop(k, before):
        reached = k < place
        new = combine(
            before, jax.tree.map(lambda part, own: part[k].astype(own.dtype), everything, shard)
        )
        return jax.tree.map(lambda a, b: jnp.where(reached, a, b), new, before)

    return lax.fori_loop(0, count, hop, start)


def prefix_2(shard, axis, combine, identity):
    count, place = (lax.axis_size(axis), lax.axis_index(axis))
    everything = jax.tree.map(
        lambda part, kind: lax.all_gather(part.astype(kind), axis),
        shard,
        jax.tree.map(lambda a: jnp.bfloat16 if a.dtype == jnp.float32 else a.dtype, shard),
    )
    start = jax.tree.map(
        lambda part, zero: jnp.broadcast_to(jnp.asarray(zero, part.dtype), part.shape),
        shard,
        identity,
    )

    def hop(k, before):
        at = count - 1 - k
        reached = at > place
        new = combine(
            before, jax.tree.map(lambda part, own: part[at].astype(own.dtype), everything, shard)
        )
        return jax.tree.map(lambda a, b: jnp.where(reached, a, b), new, before)

    return lax.fori_loop(0, count, hop, start)


def prenorm(stream, gain):
    inv_rms = lax.rsqrt(jnp.mean(stream * stream, axis=-1, keepdims=True) + epsilon)
    return stream * inv_rms * gain


def conv_act(padded, kernel, offset):
    length = padded.shape[1] - KCONV + 1
    summed = offset
    for tap_index in range(KCONV):
        summed = summed + kernel[tap_index] * padded[:, tap_index : tap_index + length]
    return jax.nn.silu(summed)


def decays(unbounded_step_size, rate_bias, log_rate):
    step_size = jax.nn.softplus(unbounded_step_size + rate_bias)
    cumul = jnp.cumsum(-jnp.exp(log_rate) * step_size, axis=2)
    return (step_size, cumul)


def mask_mix(scores, cumul, step_size):
    span = scores.shape[-1]
    causal = jnp.arange(span)[:, None] >= jnp.arange(span)[None, :]
    level_log = jnp.moveaxis(cumul, 3, 2)
    differ = level_log[..., :, None] - level_log[..., None, :]
    decay_mask = jnp.where(causal, jnp.exp(jnp.where(causal, differ, 0.0)), 0.0)
    return scores[:, :, None] * decay_mask * jnp.moveaxis(step_size, 3, 2)[..., None, :]


def state_local(inputs_x, keys_b, cumul, step_size):
    weights_end = jnp.exp(cumul[:, :, -1:, :] - cumul) * step_size
    fresh_state = jnp.einsum(
        "scthp,sctn->schpn", inputs_x * weights_end[..., None], keys_b, precision=highest_precision
    )
    block_log = cumul[:, :, -1, :]
    before = jnp.cumsum(block_log, axis=1) - block_log
    after_each = before + block_log
    total_log = jnp.sum(block_log, axis=1)
    block_count = block_log.shape[1]
    lower_mask = (jnp.arange(block_count)[:, None] > jnp.arange(block_count)[None, :])[
        None, :, :, None
    ]
    gap_log = before[:, :, None, :] - after_each[:, None, :, :]
    carry_in = jnp.where(lower_mask, jnp.exp(jnp.where(lower_mask, gap_log, 0.0)), 0.0)
    local_in = jnp.einsum("scdh,sdhpn->schpn", carry_in, fresh_state, precision=highest_precision)
    dev_state = jnp.einsum(
        "sch,schpn->shpn",
        jnp.exp(total_log[:, None, :] - after_each),
        fresh_state,
        precision=highest_precision,
    )
    return (jnp.exp(total_log), dev_state, local_in)


def state_read(queries_c, cumul, local_in, dev_in):
    block_log = cumul[:, :, -1, :]
    before = jnp.cumsum(block_log, axis=1) - block_log
    entering = local_in + jnp.exp(before)[..., None, None] * dev_in[:, None]
    return (
        jnp.einsum("sctn,schpn->scthp", queries_c, entering, precision=highest_precision)
        * jnp.exp(cumul)[..., None]
    )


def chain_join(earlier, later):
    return (earlier[0] * later[0], later[0][..., None, None] * earlier[1] + later[1])


def fetch(part_zx, part_bc, part_dt, part_out):
    return (
        lax.all_gather(part_zx, "ctx", axis=0, tiled=True),
        lax.all_gather(part_bc, "ctx", axis=0, tiled=True),
        lax.all_gather(part_dt, "ctx", axis=0, tiled=True),
        lax.all_gather(part_out, "ctx", axis=1, tiled=True),
    )


def body(
    hidden,
    out_grad,
    pre_gain,
    gate_inner_weight,
    state_maps_weight,
    step_size_weight,
    conv_x,
    bias_x,
    conv_bc,
    bias_bc,
    dt_bias,
    a_log,
    d_skip,
    norm_gain,
    output_weight,
):
    seq_count, seq_len, model_width = hidden.shape
    row_count = seq_count * seq_len
    inner_loc = gate_inner_weight.shape[3]
    heads_loc = inner_loc // HEAD_DIM
    blocks = seq_len // GROUP
    stream = hidden.astype(jnp.float32).reshape(row_count, model_width)
    kept_state = []
    for layer_index in range(LAYERS):
        weights = fetch(
            gate_inner_weight[layer_index],
            state_maps_weight[layer_index],
            step_size_weight[layer_index],
            output_weight[layer_index],
        )
        full_zx, full_bc, full_dt, full_out = weights
        normed_f, norm_pull = jax.vjp(prenorm, stream, pre_gain[layer_index])
        normalized_input = normed_f.astype(jnp.bfloat16)
        gate_and_inner = jnp.einsum(
            "rd,dkc->rkc", normalized_input, full_zx, preferred_element_type=jnp.float32
        ).astype(jnp.bfloat16)
        half_bc = jnp.dot(normalized_input, full_bc, preferred_element_type=jnp.float32).astype(
            jnp.bfloat16
        )
        unbounded_step_size = jnp.dot(
            normalized_input, full_dt, preferred_element_type=jnp.float32
        ).astype(jnp.bfloat16)
        inner_x = gate_and_inner[:, 1].reshape(seq_count, seq_len, inner_loc)
        bc_seq = half_bc.reshape(seq_count, seq_len, half_bc.shape[1])
        rim_x, rim_bc = passed_along(
            (inner_x[:, seq_len - KCONV + 1 :], bc_seq[:, seq_len - KCONV + 1 :]), "ctx", 1
        )
        padded_x = jnp.concatenate([rim_x, inner_x], axis=1).astype(jnp.float32)
        padded_bc = jnp.concatenate([rim_bc, bc_seq], axis=1).astype(jnp.float32)
        act_x, pull_x = jax.vjp(conv_act, padded_x, conv_x[layer_index], bias_x[layer_index])
        act_bc, pull_bc = jax.vjp(conv_act, padded_bc, conv_bc[layer_index], bias_bc[layer_index])
        conved_x = act_x.astype(jnp.bfloat16)
        conved_bc = lax.all_gather(act_bc.astype(jnp.bfloat16), "tensor", axis=2, tiled=True)
        (step_size, cumul), pull_decay = jax.vjp(
            decays,
            unbounded_step_size.astype(jnp.float32).reshape(seq_count, blocks, GROUP, heads_loc),
            dt_bias[layer_index],
            a_log[layer_index],
        )
        inputs_x = conved_x.reshape(seq_count, blocks, GROUP, heads_loc, HEAD_DIM)
        keys_b = conved_bc[..., :STATE].reshape(seq_count, blocks, GROUP, STATE)
        queries_c = conved_bc[..., STATE:].reshape(seq_count, blocks, GROUP, STATE)
        scores = jnp.einsum(
            "sctn,scun->sctu", queries_c, keys_b, preferred_element_type=jnp.float32
        )
        mixing_f, pull_mix = jax.vjp(mask_mix, scores, cumul, step_size)
        mixing = mixing_f.astype(jnp.bfloat16)
        within = jnp.einsum(
            "schtu,scuhp->scthp", mixing, inputs_x, preferred_element_type=jnp.float32
        )
        inputs_f = inputs_x.astype(jnp.float32)
        (dev_decay, dev_state, local_in), pull_local = jax.vjp(
            state_local, inputs_f, keys_b.astype(jnp.float32), cumul, step_size
        )
        identity = (jnp.ones_like(dev_decay), jnp.zeros_like(dev_state))
        dev_in = prefix((dev_decay, dev_state), "ctx", chain_join, identity)[1]
        carried, pull_read = jax.vjp(
            state_read, queries_c.astype(jnp.float32), cumul, local_in, dev_in
        )
        ssd_heads = within + carried + d_skip[layer_index][:, None] * inputs_f
        ssd_out = ssd_heads.reshape(row_count, inner_loc)
        gate_z = gate_and_inner[:, 0].astype(jnp.float32)
        silu_z = jax.nn.silu(gate_z)
        gated_y = ssd_out * silu_z
        square_sum = lax.psum(jnp.sum(gated_y * gated_y, axis=1), "tensor")
        inv_rms = lax.rsqrt(square_sum / DI + epsilon)[:, None]
        normed_y = gated_y * inv_rms
        gated_output = (normed_y * norm_gain[layer_index]).astype(jnp.bfloat16)
        mixer_branch = lax.psum(
            jnp.dot(gated_output, full_out, preferred_element_type=jnp.float32), "tensor"
        )
        kept_state.append(
            (
                weights,
                norm_pull,
                normalized_input,
                gate_and_inner,
                pull_x,
                pull_bc,
                pull_decay,
                inputs_x,
                keys_b,
                queries_c,
                pull_mix,
                mixing,
                inputs_f,
                dev_decay,
                dev_in,
                pull_local,
                identity,
                pull_read,
                ssd_out,
                gate_z,
                silu_z,
                gated_y,
                inv_rms,
                normed_y,
                gated_output,
            )
        )
        stream = stream + mixer_branch
    output = stream.reshape(seq_count, seq_len, model_width)
    stream_grad = out_grad.astype(jnp.float32).reshape(row_count, model_width)
    big_grads = [None] * LAYERS
    small_grads = [None] * LAYERS
    for layer_index in reversed(range(LAYERS)):
        (
            weights,
            norm_pull,
            normalized_input,
            gate_and_inner,
            pull_x,
            pull_bc,
            pull_decay,
            inputs_x,
            keys_b,
            queries_c,
            pull_mix,
            mixing,
            inputs_f,
            dev_decay,
            dev_in,
            pull_local,
            identity,
            pull_read,
            ssd_out,
            gate_z,
            silu_z,
            gated_y,
            inv_rms,
            normed_y,
            gated_output,
        ) = kept_state[layer_index]
        full_zx, full_bc, full_dt, full_out = fetch(
            gate_inner_weight[layer_index],
            state_maps_weight[layer_index],
            step_size_weight[layer_index],
            output_weight[layer_index],
        )
        grad_b = stream_grad.astype(jnp.bfloat16)
        grad_out_w = jnp.einsum(
            "rc,rd->cd", gated_output, grad_b, preferred_element_type=jnp.float32
        )
        d_gate_out = jnp.einsum("rd,cd->rc", grad_b, full_out, preferred_element_type=jnp.float32)
        grad_norm = jnp.sum(d_gate_out * normed_y, axis=0)
        d_norm = d_gate_out * norm_gain[layer_index]
        cross_sum = lax.psum(jnp.sum(d_norm * gated_y, axis=1), "tensor")
        d_gated = (
            inv_rms * d_norm - gated_y * (inv_rms * inv_rms * inv_rms) * (cross_sum / DI)[:, None]
        )
        sig_z = jax.nn.sigmoid(gate_z)
        d_gate_z = d_gated * ssd_out * sig_z * (1.0 + gate_z * (1.0 - sig_z))
        d_heads = (d_gated * silu_z).astype(jnp.bfloat16).reshape(inputs_x.shape)
        d_heads_f = d_heads.astype(jnp.float32)
        grad_skip = jnp.sum(d_heads_f * inputs_f, axis=(0, 1, 2, 4))
        d_queries, d_cumul, d_local, d_dev_in = pull_read(d_heads_f)
        later_grad = prefix_2((dev_decay, d_dev_in), "ctx", chain_join, identity)[1]
        d_dev_decay = jnp.sum(later_grad * dev_in, axis=(2, 3))
        d_inputs, d_keys, d_cumul_b, d_step = pull_local((d_dev_decay, later_grad, d_local))
        d_mixing = jnp.einsum(
            "scthp,scuhp->schtu", d_heads, inputs_x, preferred_element_type=jnp.float32
        )
        d_inputs = (
            d_inputs
            + d_skip[layer_index][:, None] * d_heads_f
            + jnp.einsum("schtu,scthp->scuhp", mixing, d_heads, preferred_element_type=jnp.float32)
        )
        d_scores, d_cumul_c, d_step_c = pull_mix(d_mixing)
        d_scores_b = d_scores.astype(jnp.bfloat16)
        d_queries = d_queries + jnp.einsum(
            "sctu,scun->sctn", d_scores_b, keys_b, preferred_element_type=jnp.float32
        )
        d_keys = d_keys + jnp.einsum(
            "sctu,sctn->scun", d_scores_b, queries_c, preferred_element_type=jnp.float32
        )
        d_raw, grad_rate_bias, grad_log_rate = pull_decay(
            (d_step + d_step_c, d_cumul + d_cumul_b + d_cumul_c)
        )
        d_bc_full = jnp.concatenate([d_keys, d_queries], axis=-1).reshape(
            seq_count, seq_len, 2 * STATE
        )
        d_bc_half = lax.psum_scatter(
            d_bc_full.astype(jnp.bfloat16), "tensor", scatter_dimension=2, tiled=True
        ).astype(jnp.float32)
        d_pad_x, grad_conv_x, grad_bias_x = pull_x(d_inputs.reshape(seq_count, seq_len, inner_loc))
        d_pad_bc, grad_conv_bc, grad_bias_bc = pull_bc(d_bc_half)
        back_x, back_bc = passed_along(
            (d_pad_x[:, : KCONV - 1], d_pad_bc[:, : KCONV - 1]), "ctx", -1
        )
        d_inner = d_pad_x[:, KCONV - 1 :].at[:, seq_len - KCONV + 1 :].add(back_x)
        d_bc_in = d_pad_bc[:, KCONV - 1 :].at[:, seq_len - KCONV + 1 :].add(back_bc)
        d_zx = jnp.stack([d_gate_z, d_inner.reshape(row_count, inner_loc)], axis=1).astype(
            jnp.bfloat16
        )
        d_bc_b = d_bc_in.reshape(row_count, d_bc_in.shape[2]).astype(jnp.bfloat16)
        d_dt_b = d_raw.reshape(row_count, heads_loc).astype(jnp.bfloat16)
        d_normed_part = (
            jnp.einsum("rkc,dkc->rd", d_zx, full_zx, preferred_element_type=jnp.float32)
            + jnp.einsum("rn,dn->rd", d_bc_b, full_bc, preferred_element_type=jnp.float32)
            + jnp.einsum("rh,dh->rd", d_dt_b, full_dt, preferred_element_type=jnp.float32)
        )
        d_normed = lax.psum(d_normed_part.astype(jnp.bfloat16), "tensor").astype(jnp.float32)
        grad_zx = jnp.einsum(
            "rd,rkc->dkc", normalized_input, d_zx, preferred_element_type=jnp.float32
        )
        grad_bc = jnp.einsum(
            "rd,rn->dn", normalized_input, d_bc_b, preferred_element_type=jnp.float32
        )
        grad_dt = jnp.einsum(
            "rd,rh->dh", normalized_input, d_dt_b, preferred_element_type=jnp.float32
        )
        d_stream, grad_pre = norm_pull(d_normed)
        stream_grad = stream_grad + d_stream
        shards = (
            lax.psum_scatter(
                grad_zx.astype(jnp.bfloat16), "ctx", scatter_dimension=0, tiled=True
            ).astype(jnp.float32),
            lax.psum_scatter(
                grad_bc.astype(jnp.bfloat16), "ctx", scatter_dimension=0, tiled=True
            ).astype(jnp.float32),
            lax.psum_scatter(
                grad_dt.astype(jnp.bfloat16), "ctx", scatter_dimension=0, tiled=True
            ).astype(jnp.float32),
            lax.psum_scatter(
                grad_out_w.astype(jnp.bfloat16), "ctx", scatter_dimension=1, tiled=True
            ).astype(jnp.float32),
        )
        big_grads[layer_index] = (
            lax.psum(shards[0].astype(jnp.bfloat16), "dp").astype(jnp.float32),
            lax.psum(shards[1].astype(jnp.bfloat16), "dp").astype(jnp.float32),
            lax.psum(shards[2].astype(jnp.bfloat16), "dp").astype(jnp.float32),
            lax.psum(shards[3].astype(jnp.bfloat16), "dp").astype(jnp.float32),
        )
        small_grads[layer_index] = (
            grad_pre,
            grad_conv_x,
            grad_bias_x,
            grad_conv_bc,
            grad_bias_bc,
            grad_rate_bias,
            grad_log_rate,
            grad_skip,
            grad_norm,
        )
    stacked_small = tuple(
        (
            jnp.stack([small_grads[layer_index][member] for layer_index in range(LAYERS)])
            for member in range(9)
        )
    )
    summed_small = lax.psum(
        (
            stacked_small[0],
            stacked_small[1],
            stacked_small[2],
            stacked_small[3],
            stacked_small[4],
            stacked_small[5],
            stacked_small[6],
            stacked_small[7],
            stacked_small[8],
        ),
        ("dp", "ctx"),
    )
    stacked_big = tuple(
        (
            jnp.stack([big_grads[layer_index][member] for layer_index in range(LAYERS)])
            for member in range(4)
        )
    )
    grad_hidden = stream_grad.reshape(seq_count, seq_len, model_width)
    return (
        output,
        grad_hidden,
        summed_small[0],
        stacked_big[0],
        stacked_big[1],
        stacked_big[2],
        summed_small[1],
        summed_small[2],
        summed_small[3],
        summed_small[4],
        summed_small[5],
        summed_small[6],
        summed_small[7],
        summed_small[8],
        stacked_big[3],
    )


def solution(mesh):
    return jax.shard_map(
        body,
        mesh=mesh,
        in_specs=(
            P("dp", "ctx", None),
            P("dp", "ctx", None),
            P(),
            P(None, "ctx", None, "tensor"),
            P(None, "ctx", "tensor"),
            P(None, "ctx", "tensor"),
            P(None, None, "tensor"),
            P(None, "tensor"),
            P(None, None, "tensor"),
            P(None, "tensor"),
            P(None, "tensor"),
            P(None, "tensor"),
            P(None, "tensor"),
            P(None, "tensor"),
            P(None, "tensor", "ctx"),
        ),
        out_specs=(
            P("dp", "ctx", None),
            P("dp", "ctx", None),
            P(),
            P(None, "ctx", None, "tensor"),
            P(None, "ctx", "tensor"),
            P(None, "ctx", "tensor"),
            P(None, None, "tensor"),
            P(None, "tensor"),
            P(None, None, "tensor"),
            P(None, "tensor"),
            P(None, "tensor"),
            P(None, "tensor"),
            P(None, "tensor"),
            P(None, "tensor"),
            P(None, "tensor", "ctx"),
        ),
        check_vma=False,
    )
```

profile of v0, /device:TPU:0, one launch (start us, length us, event | category | flops | bytes accessed | tf_op | source)
XLA Modules:
  0.0 1323.4 jit_solution(6104226263722451918)
XLA Ops:
  14.5 10.7 all-gather.1
  32.3 7.4 all-gather.2
  53.5 14.3 %all-gather.25.cloned.1.call-done = bf16[1,1024,2,1024]{3,1,2,0:T(8,128)(2,1)} async-done(((bf16[1,256,2,1024]{3,1,2,0:T(8,128)(2,1)}), bf16[1,1024,2,1024]{3,1,2,0:T(8,128)(2,1)}) %all-gather.25.cloned.1.call-update) | async-done | bytes 4194320 | tf_op jit(solution)/shard_map/all_gather | solution.py:140
  67.9 7.3 fusion.83
  88.8 10.1 collective-permute-done
  116.7 8.2 fusion.204
  131.4 10.2 all-gather.14
  148.5 7.3 reshape.946
  155.8 7.7 copy.535
  163.6 11.5 fusion.206
  175.1 7.9 while.64
  187.1 8.1 multiply_reduce_fusion.18
  195.3 8.2 copy.674
  203.4 7.8 reshape.945
  214.8 8.2 fusion.97
  225.7 7.9 all-gather.8
  233.6 8.4 all-gather.7
  242.0 9.7 all-reduce.47.cloned.1.call-done
  261.2 46.4 %all-gather.31.cloned.1.call-done = bf16[1,1024,2,1024]{3,1,2,0:T(8,128)(2,1)} async-done(((bf16[1,256,2,1024]{3,1,2,0:T(8,128)(2,1)}), bf16[1,1024,2,1024]{3,1,2,0:T(8,128)(2,1)}) %all-gather.31.cloned.1.call-update) | async-done | bytes 4194320 | tf_op jit(solution)/shard_map/all_gather | solution.py:140
  331.4 7.0 collective-permute-done.3
  354.1 8.2 fusion.197
  364.0 9.8 all-gather.15
  374.6 7.7 reshape.948
  382.3 7.9 copy.557
  395.7 11.5 fusion.199
  416.3 9.3 multiply_reduce_fusion.16
  425.6 8.2 copy.677
  433.8 7.6 reshape.947
  444.1 9.7 multiply_reduce_fusion.4
  456.3 9.0 fusion.48
  490.3 14.8 %fusion.9 = (f32[2,2,16,256]{3,2,1,0:T(8,128)}, f32[2,2,16,256]{3,2,1,0:T(8,128)}, f32[2,2,16,256]{3,2,1,0:T(8,128)}, bf16[2,2,256,256]{3,2,1,0:T(8,128)(2,1)S(1)}) fusion(f32[2,2,16,256]{3,2,1,0:T(8,128)S(1)} %get-tuple-element.858, f32[2,2,16,256]{3,2,1,0:T(8,128)S(1)} %get-tuple-element.864, f32[2,2,256,256]{3,2,1,0:T(8,128)} %fusion.312, ...), kind=kOutput, calls=%fused_computation.27 | convolution fusion | flops 599474176 | bytes 6160384 | tf_op jit(solution)/shard_map/scthp,scuhp->schtu/dot_general | solution.py:327
  507.3 21.7 %fusion.293 = (f32[2,2,16]{1,2,0:T(8,128)}, f32[2,2,16]{1,2,0:T(8,128)}) fusion(f32[2,2,16]{1,2,0:T(8,128)S(1)} %copy-done.126, f32[2,2,16]{1,2,0:T(8,128)S(1)} %bitcast.837, f32[2,2,16,64,128]{4,3,2,1,0:T(8,128)S(1)} %copy-done.50, f32[2,16,64,128,2]{3,2,1,4,0:T(8,128)S(1)} %bitcast.805, pred[2,2]{1,0:T(4,128)(4,1)S(1)} %copy-done.214), kind=kOutput, calls=%fused_computation.543 | convolution fusion | flops 12583680 | bytes 4195332 | tf_op jit(solution)/shard_map/transpose(jvp(scdh,sdhpn->schpn))/dot_general | solution.py:114
  529.0 10.2 while.66
  539.3 11.6 add_bitcast_fusion.1
  561.8 8.5 fusion.37
  582.0 12.5 multiply_reduce_fusion.9
  604.3 19.7 %fusion.195 = f32[2,16,1,2,1]{3,2,4,1,0:T(1,128)S(1)} fusion(f32[2,16,64,128,1]{3,4,2,1,0:T(1,128)S(1)} %bitcast.762, f32[2,2,16,64,128]{4,3,2,1,0:T(8,128)} %copy-done.49), kind=kOutput, calls=%fused_computation.306 | convolution fusion | flops 6291456 | bytes 3145984 | tf_op jit(solution)/shard_map/transpose(jvp(sch,schpn->shpn))/dot_general | solution.py:115
  625.4 9.9 reduce-window.34
  639.9 7.2 pad_add_fusion.1
  661.6 10.0 fusion.60
  686.5 7.7 fusion.89
  698.9 10.5 all-reduce.51.cloned.1.call-done
  714.3 28.0 %all-reduce.49.cloned.1.call-done = f32[1024,1024]{1,0:T(8,128)} async-done(((f32[1024,1024]{1,0:T(8,128)}), f32[1024,1024]{1,0:T(8,128)}) %all-reduce.49.cloned.1.call-update) | async-done | bytes 4194320 | tf_op jit(solution)/shard_map/psum | solution.py:236
  760.9 8.6 fusion.49
  790.0 14.6 %fusion.11 = (f32[2,2,16,256]{3,2,1,0:T(8,128)}, f32[2,2,16,256]{3,2,1,0:T(8,128)}, f32[2,2,16,256]{3,2,1,0:T(8,128)}, bf16[2,2,256,256]{3,2,1,0:T(8,128)(2,1)S(1)}) fusion(f32[2,2,16,256]{3,2,1,0:T(8,128)S(1)} %copy-done.128, f32[2,2,16,256]{3,2,1,0:T(8,128)} %get-tuple-element.868, f32[2,2,256,256]{3,2,1,0:T(8,128)S(1)} %copy-done.80, ...), kind=kOutput, calls=%fused_computation.29 | convolution fusion | flops 599474176 | bytes 6160384 | tf_op jit(solution)/shard_map/scthp,scuhp->schtu/dot_general | solution.py:327
  804.9 14.8 %all-gather.39.cloned.1.call-done = bf16[8,16,64,128]{3,2,1,0:T(8,128)(2,1)} async-done(((bf16[2,16,64,128]{3,2,1,0:T(8,128)(2,1)}), bf16[8,16,64,128]{3,2,1,0:T(8,128)(2,1)}) %all-gather.39.cloned.1.call-update) | async-done | bytes 2097168 | tf_op jit(solution)/shard_map/all_gather | solution.py:50
  819.8 7.9 while.67
  827.8 12.1 add_bitcast_fusion
  862.6 8.6 convolution_convert_fusion.1
  890.0 9.5 fusion.81
  916.0 7.0 reshape.859
  922.9 12.6 multiply_reduce_fusion.13
  947.3 8.3 pad_add_fusion
  973.6 9.5 fusion.82
  990.7 21.3 %fusion.292 = (f32[2,2,16]{1,2,0:T(8,128)S(1)}, f32[2,2,16]{1,2,0:T(8,128)S(1)}) fusion(f32[2,2,16]{1,2,0:T(8,128)S(1)} %copy-done.124, f32[2,2,16]{1,2,0:T(8,128)S(1)} %bitcast.834, f32[2,2,16,64,128]{4,3,2,1,0:T(8,128)S(1)} %copy-done.48, f32[2,16,64,128,2]{3,2,1,4,0:T(8,128)S(1)} %bitcast.803, pred[2,2]{1,0:T(4,128)(4,1)S(1)} %copy-done.216), kind=kOutput, calls=%fused_computation.542 | convolution fusion | flops 12583680 | bytes 4195332 | tf_op jit(solution)/shard_map/transpose(jvp(scdh,sdhpn->schpn))/dot_general | solution.py:114
  1014.0 20.1 %fusion.202 = f32[2,16,1,2,1]{3,2,4,1,0:T(1,128)S(1)} fusion(f32[2,16,64,128,1]{3,4,2,1,0:T(1,128)} %bitcast.763, f32[2,2,16,64,128]{4,3,2,1,0:T(8,128)} %copy-done.47), kind=kOutput, calls=%fused_computation.313 | convolution fusion | flops 6291456 | bytes 3145984 | tf_op jit(solution)/shard_map/transpose(jvp(sch,schpn->shpn))/dot_general | solution.py:115
  1035.4 9.9 reduce-window.36
  1049.8 7.8 fusion.70
  1060.1 39.0 %reduce-scatter.15.cloned.1.call-done = bf16[256,2,1024]{2,0,1:T(8,128)(2,1)} async-done(((bf16[1024,2,1024]{2,0,1:T(8,128)(2,1)}), bf16[256,2,1024]{2,0,1:T(8,128)(2,1)}) %reduce-scatter.15.cloned.1.call-update) | async-done | bytes 1048592 | tf_op jit(solution)/shard_map/reduce_scatter | solution.py:382
  1099.9 25.0 %reduce-scatter.25.cloned.1.call-done = bf16[256,16]{0,1:T(8,128)(2,1)} async-done(((bf16[1024,16]{0,1:T(8,128)(2,1)}), bf16[256,16]{0,1:T(8,128)(2,1)}) %reduce-scatter.25.cloned.1.call-update) | async-done | bytes 8208 | tf_op jit(solution)/shard_map/reduce_scatter | solution.py:388
  1124.9 26.0 %reduce-scatter.23.cloned.1.call-done = bf16[256,16]{0,1:T(8,128)(2,1)} async-done(((bf16[1024,16]{0,1:T(8,128)(2,1)}), bf16[256,16]{0,1:T(8,128)(2,1)}) %reduce-scatter.23.cloned.1.call-update) | async-done | bytes 8208 | tf_op jit(solution)/shard_map/reduce_scatter | solution.py:388
  1150.9 19.4 %all-reduce.39 = (bf16[1,256,16]{1,2,0:T(8,128)(2,1)S(1)}, bf16[1,256,16]{1,2,0:T(8,128)(2,1)S(1)}) all-reduce(bf16[1,256,16]{1,2,0:T(8,128)(2,1)} %bitcast.892, bf16[1,256,16]{1,2,0:T(8,128)(2,1)} %bitcast.893), channel_id=1, replica_groups=mesh['dp'=4,'ctx'=4,'tensor'=2] {'dp'}, use_global_device_ids=true, to_apply=%region_82.84 | all-reduce | flops 8192 | bytes 32768 | tf_op jit(solution)/shard_map/psum | solution.py:398
  1178.6 81.5 %all-reduce.38 = (f32[2,1024]{1,0:T(2,128)}, f32[2,4,1024]{2,1,0:T(4,128)}, f32[2,1024]{1,0:T(2,128)}, f32[2,4,128]{2,1,0:T(4,128)}, f32[2,128]{1,0:T(2,128)}, /...) all-reduce(f32[2,1024]{1,0:T(2,128)S(1)} %pad_maximum_fusion.13, ...), channel_id=1, replica_groups=mesh['dp'=4,'ctx'=4,'tensor'=2] {'dp','ctx'}, use_global_device_ids=true, to_apply=%region_70.72 | all-reduce | flops 15712 | bytes 125696 | tf_op jit(solution)/shard_map/psum | solution.py:418
  1264.9 42.5 %all-reduce.55.cloned.1.call-done = (bf16[1,256,2,1024]{3,1,2,0:T(8,128)(2,1)}, bf16[1,256,2,1024]{3,1,2,0:T(8,128)(2,1)}, bf16[1,256,128]{2,1,0:T(8,128)(2,1)},...) async-done(((bf16[1,256,2,1024]{3,1,2,0:T(8,128)(2,1)}, bf16[1,256,2,1024]{3,1,2,0:T(8,128)(2,1)}, ...) | async-done | bytes 3276816 | tf_op jit(solution)/shard_map/psum | solution.py:396
  (894 shorter events, 454.7 us)
Async XLA Ops:
  7.2 60.6 %all-gather.25.cloned.1.call-start = ((), (), s32[]{:S(2)}) async-start(), calls=%async_computation.22 | async-start | bytes 5242880 | tf_op jit(solution)/shard_map/all_gather | solution.py:140
  12.1 163.0 %all-gather.27.cloned.1.call-start = ((), (), s32[]{:S(2)}) async-start(), calls=%async_computation.23 | async-start | bytes 2621440 | tf_op jit(solution)/shard_map/all_gather | solution.py:27
  27.2 22.1 %collective-permute-start.1 = (bf16[2,3,128]{2,1,0:T(4,128)(2,1)S(1)}, bf16[2,3,128]{2,1,0:T(4,128)(2,1)S(1)}, u32[]{:S(2)}, u32[]{:S(2)}) collective-permute-start(bf16[2,3,128]{2,1,0:T(4,128)(2,1)S(1)} %slice.498), channel_id=1, source_target_pairs={{0,2},{2,4},{4,6},{1,3},{3,5},{5,7},{8,10},{10,12},{12,14},{9,11},... | collective-permute-start | bytes 4616 | tf_op jit(solution)/shard_map/ppermute | solution.py:21
  45.7 83.1 %copy-start.208 = (f32[2,16]{1,0:T(2,128)}, f32[2,16]{1,0:T(2,128)S(1)}, u32[]{:S(2)}) copy-start(f32[2,16]{1,0:T(2,128)S(1)} %get-tuple-element.731) | copy-start | bytes 388
  48.0 53.7 %copy-start.157 = (f32[1,1,1024]{2,1,0:T(1,128)}, f32[1,1,1024]{2,1,0:T(1,128)S(1)}, u32[]{:S(2)}) copy-start(f32[1,1,1024]{2,1,0:T(1,128)S(1)} %get-tuple-element.877) | copy-start | bytes 12292
  48.0 53.7 %copy-start.159 = (f32[1,1,1024]{2,1,0:T(1,128)}, f32[1,1,1024]{2,1,0:T(1,128)S(1)}, u32[]{:S(2)}) copy-start(f32[1,1,1024]{2,1,0:T(1,128)S(1)} %get-tuple-element.878) | copy-start | bytes 12292
  48.0 53.7 %copy-start.161 = (f32[1,1,1024]{2,1,0:T(1,128)}, f32[1,1,1024]{2,1,0:T(1,128)S(1)}, u32[]{:S(2)}) copy-start(f32[1,1,1024]{2,1,0:T(1,128)S(1)} %get-tuple-element.879) | copy-start | bytes 12292
  48.0 53.7 %copy-start.163 = (f32[1,1,1024]{2,1,0:T(1,128)}, f32[1,1,1024]{2,1,0:T(1,128)S(1)}, u32[]{:S(2)}) copy-start(f32[1,1,1024]{2,1,0:T(1,128)S(1)} %get-tuple-element.880) | copy-start | bytes 12292
  48.6 66.7 %copy-start.104 = (f32[2,2,16]{1,2,0:T(8,128)}, f32[2,2,16]{1,2,0:T(8,128)S(1)}, u32[]{:S(2)}) copy-start(f32[2,2,16]{1,2,0:T(8,128)S(1)} %get-tuple-element.816) | copy-start | bytes 772
  48.6 115.0 %copy-start.122 = (f32[2,2,16]{1,2,0:T(8,128)}, f32[2,2,16]{1,2,0:T(8,128)S(1)}, u32[]{:S(2)}) copy-start(f32[2,2,16]{1,2,0:T(8,128)S(1)} %get-tuple-element.817) | copy-start | bytes 772
  48.7 62.7 %copy-start.95 = (f32[2,2,256,16]{2,3,1,0:T(8,128)}, f32[2,2,256,16]{2,3,1,0:T(8,128)S(1)}, u32[]{:S(2)}) copy-start(f32[2,2,256,16]{2,3,1,0:T(8,128)S(1)} %get-tuple-element.867) | copy-start | bytes 196612
  48.8 138.2 %copy-start.83 = (f32[2,2,256,16]{2,3,1,0:T(8,128)}, f32[2,2,256,16]{2,3,1,0:T(8,128)S(1)}, u32[]{:S(2)}) copy-start(f32[2,2,256,16]{2,3,1,0:T(8,128)S(1)} %get-tuple-element.866) | copy-start | bytes 196612
  84.3 14.5 %collective-permute-start = (bf16[2,3,1024]{1,2,0:T(8,128)(2,1)S(1)}, bf16[2,3,1024]{1,2,0:T(8,128)(2,1)S(1)}, u32[]{:S(2)}, u32[]{:S(2)}) collective-permute-start(bf16[2,3,1024]{1,2,0:T(8,128)(2,1)S(1)} %slice.493), channel_id=1, source_target_pairs={{0,2},{2,4},{4,6},{1,3},{3,5},{5,7},{8,10},{10,12},{12,14},{9,11},... | collective-permute-start | bytes 36872 | tf_op jit(solution)/shard_map/ppermute | solution.py:21
  88.8 57.5 %copy-start.52 = (bf16[2,512,128]{2,1,0:T(8,128)(2,1)}, bf16[2,512,128]{2,1,0:T(8,128)(2,1)S(1)}, u32[]{:S(2)}) copy-start(bf16[2,512,128]{2,1,0:T(8,128)(2,1)S(1)} %get-tuple-element.852) | copy-start | bytes 786436
  125.8 88.4 %all-gather.29.cloned.1.call-start = ((), (), s32[]{:S(2)}) async-start(), calls=%async_computation.24 | async-start | bytes 2621440 | tf_op jit(solution)/shard_map/all_gather | solution.py:143
  128.1 123.6 %all-reduce.47.cloned.1.call-start = ((), (), s32[]{:S(2)}) async-start(), calls=%async_computation.10 | async-start | bytes 8388608 | tf_op jit(solution)/shard_map/psum | solution.py:236
  223.1 84.5 %all-gather.31.cloned.1.call-start = ((), (), s32[]{:S(2)}) async-start(), calls=%async_computation.25 | async-start | bytes 5242880 | tf_op jit(solution)/shard_map/all_gather | solution.py:140
  225.6 181.6 %all-gather.33.cloned.1.call-start = ((), (), s32[]{:S(2)}) async-start(), calls=%async_computation.26 | async-start | bytes 2621440 | tf_op jit(solution)/shard_map/all_gather | solution.py:27
  242.0 85.3 %copy-start.66 = (bf16[1,1024,128]{2,1,0:T(8,128)(2,1)}, bf16[1,1024,128]{2,1,0:T(8,128)(2,1)S(1)}, u32[]{:S(2)}) copy-start(bf16[1,1024,128]{2,1,0:T(8,128)(2,1)S(1)} %all-gather.7) | copy-start | bytes 786436
  257.0 70.3 %copy-start.6 = (bf16[1024,1024]{1,0:T(8,128)(2,1)}, bf16[1024,1024]{1,0:T(8,128)(2,1)S(1)}, u32[]{:S(2)}) copy-start(bf16[1024,1024]{1,0:T(8,128)(2,1)S(1)} %multiply_convert_fusion.11) | copy-start | bytes 6291460
  257.7 56.8 %copy-start.72 = (f32[2,2,256,16]{2,1,0,3:T(2,128)}, f32[2,2,256,16]{2,1,0,3:T(2,128)S(1)}, u32[]{:S(2)}) copy-start(f32[2,2,256,16]{2,1,0,3:T(2,128)S(1)} %reshape.879) | copy-start | bytes 196612
  257.9 232.4 %copy-start.134 = (f32[2,2,16,256]{3,2,1,0:T(8,128)}, f32[2,2,16,256]{3,2,1,0:T(8,128)S(1)}, u32[]{:S(2)}) copy-start(f32[2,2,16,256]{3,2,1,0:T(8,128)S(1)} %get-tuple-element.858) | copy-start | bytes 196612
  260.2 54.4 %copy-start.62 = (f32[2,2,16,2,128]{4,2,3,1,0:T(8,128)}, f32[2,2,16,2,128]{4,2,3,1,0:T(8,128)S(1)}, u32[]{:S(2)}) copy-start(f32[2,2,16,2,128]{4,2,3,1,0:T(8,128)S(1)} %reduce-window.30) | copy-start | bytes 196612
  260.4 54.2 %copy-start.102 = (f32[2,2,16,2]{2,3,1,0:T(2,128)}, f32[2,2,16,2]{2,3,1,0:T(2,128)S(1)}, u32[]{:S(2)}) copy-start(f32[2,2,16,2]{2,3,1,0:T(2,128)S(1)} %slice.523) | copy-start | bytes 1540
  260.5 229.7 %copy-start.135 = (f32[2,2,16,256]{3,2,1,0:T(8,128)}, f32[2,2,16,256]{3,2,1,0:T(8,128)S(1)}, u32[]{:S(2)}) copy-start(f32[2,2,16,256]{3,2,1,0:T(8,128)S(1)} %get-tuple-element.864) | copy-start | bytes 196612
  260.7 53.9 %copy-start.113 = (f32[2,2,16]{2,1,0:T(2,128)}, f32[2,2,16]{2,1,0:T(2,128)S(1)}, u32[]{:S(2)}) copy-start(f32[2,2,16]{2,1,0:T(2,128)S(1)} %get-tuple-element.730) | copy-start | bytes 772
  260.7 103.3 %copy-start.210 = (f32[2,16]{1,0:T(2,128)}, f32[2,16]{1,0:T(2,128)S(1)}, u32[]{:S(2)}) copy-start(f32[2,16]{1,0:T(2,128)S(1)} %get-tuple-element.729) | copy-start | bytes 388
  261.2 289.6 %copy-start.97 = (f32[2,2,256,16]{2,3,1,0:T(8,128)}, f32[2,2,256,16]{2,3,1,0:T(8,128)S(1)}, u32[]{:S(2)}) copy-start(f32[2,2,256,16]{2,3,1,0:T(8,128)S(1)} %get-tuple-element.863) | copy-start | bytes 196612
  323.7 18.3 %collective-permute-start.2 = (bf16[2,3,1024]{1,2,0:T(8,128)(2,1)S(1)}, bf16[2,3,1024]{1,2,0:T(8,128)(2,1)S(1)}, u32[]{:S(2)}, u32[]{:S(2)}) collective-permute-start(bf16[2,3,1024]{1,2,0:T(8,128)(2,1)S(1)} %slice.510), channel_id=1, source_target_pairs={{0,2},{2,4},{4,6},{1,3},{3,5},{5,7},{8,10},{10,12},{12,14},{9,11},... | collective-permute-start | bytes 36872 | tf_op jit(solution)/shard_map/ppermute | solution.py:21
  328.0 10.4 collective-permute-start.3
  331.4 64.2 %copy-start.125 = (f32[2,2,16]{1,2,0:T(8,128)}, f32[2,2,16]{1,2,0:T(8,128)S(1)}, u32[]{:S(2)}) copy-start(f32[2,2,16]{1,2,0:T(8,128)S(1)} %get-tuple-element.809) | copy-start | bytes 772
  363.2 80.9 %all-gather.35.cloned.1.call-start = ((), (), s32[]{:S(2)}) async-start(), calls=%async_computation.27 | async-start | bytes 2621440 | tf_op jit(solution)/shard_map/all_gather | solution.py:143
  364.0 165.1 %all-gather.37.cloned.1.call-start = ((), (), s32[]{:S(2)}) async-start(), calls=%async_computation.28 | async-start | bytes 2621440 | tf_op jit(solution)/shard_map/all_gather | solution.py:50
  488.8 182.9 %reduce-scatter.31.cloned.1.call-start = ((), (), s32[]{:S(2)}) async-start(), calls=%async_computation.30 | async-start | bytes 786432
  561.8 147.7 %all-reduce.51.cloned.1.call-start = ((), (), s32[]{:S(2)}) async-start(), calls=%async_computation.12 | async-start | bytes 4194304 | tf_op jit(solution)/shard_map/psum | solution.py:369
  602.7 45.5 %collective-permute-start.4 = (f32[2,3,1024]{2,0,1:T(2,128)S(1)}, f32[2,3,1024]{2,0,1:T(2,128)}, u32[]{:S(2)}, u32[]{:S(2)}) collective-permute-start(f32[2,3,1024]{2,0,1:T(2,128)S(1)} %copy.566), channel_id=1, source_target_pairs={{2,0},{4,2},{6,4},{3,1},{5,3},{7,5},{10,8},{12,10},{14,12},{11,9},... | collective-permute-start | bytes 73736 | tf_op jit(solution)/shard_map/ppermute | solution.py:21
  674.3 6.3 collective-permute-start.5
  686.4 55.9 %all-reduce.49.cloned.1.call-start = ((), (), s32[]{:S(2)}) async-start(), calls=%async_computation.11 | async-start | bytes 8388608 | tf_op jit(solution)/shard_map/psum | solution.py:236
  694.2 125.5 %all-gather.39.cloned.1.call-start = ((), (), s32[]{:S(2)}) async-start(), calls=%async_computation.29 | async-start | bytes 2621440 | tf_op jit(solution)/shard_map/all_gather | solution.py:50
  783.0 90.2 %reduce-scatter.33.cloned.1.call-start = ((), (), s32[]{:S(2)}) async-start(), calls=%async_computation.31 | async-start | bytes 786432
  846.0 214.0 %reduce-scatter.29.cloned.1.call-start = ((), (), s32[]{:S(2)}) async-start(), calls=%async_computation.21 | async-start | bytes 2621440 | tf_op jit(solution)/shard_map/reduce_scatter | solution.py:391
  859.9 200.2 %reduce-scatter.21.cloned.1.call-start = ((), (), s32[]{:S(2)}) async-start(), calls=%async_computation.17 | async-start | bytes 327680 | tf_op jit(solution)/shard_map/reduce_scatter | solution.py:385
  862.4 197.7 %reduce-scatter.27.cloned.1.call-start = ((), (), s32[]{:S(2)}) async-start(), calls=%async_computation.20 | async-start | bytes 2621440 | tf_op jit(solution)/shard_map/reduce_scatter | solution.py:391
  871.3 188.8 %reduce-scatter.19.cloned.1.call-start = ((), (), s32[]{:S(2)}) async-start(), calls=%async_computation.16 | async-start | bytes 327680 | tf_op jit(solution)/shard_map/reduce_scatter | solution.py:385
  880.0 5.5 collective-permute-start.7
  890.0 170.2 %reduce-scatter.17.cloned.1.call-start = ((), (), s32[]{:S(2)}) async-start(), calls=%async_computation.15 | async-start | bytes 5242880 | tf_op jit(solution)/shard_map/reduce_scatter | solution.py:382
  899.5 199.6 %reduce-scatter.15.cloned.1.call-start = ((), (), s32[]{:S(2)}) async-start(), calls=%async_computation.14 | async-start | bytes 5242880 | tf_op jit(solution)/shard_map/reduce_scatter | solution.py:382
  946.0 12.2 collective-permute-start.6
  983.1 141.9 %reduce-scatter.25.cloned.1.call-start = ((), (), s32[]{:S(2)}) async-start(), calls=%async_computation.19 | async-start | bytes 40960 | tf_op jit(solution)/shard_map/reduce_scatter | solution.py:388
  986.4 164.6 %reduce-scatter.23.cloned.1.call-start = ((), (), s32[]{:S(2)}) async-start(), calls=%async_computation.18 | async-start | bytes 40960 | tf_op jit(solution)/shard_map/reduce_scatter | solution.py:388
  1049.7 125.5 %all-reduce.53.cloned.1.call-start = ((), (), s32[]{:S(2)}) async-start(), calls=%async_computation.13 | async-start | bytes 4194304 | tf_op jit(solution)/shard_map/psum | solution.py:369
  1059.8 40.1 %copy-start.200 = (f32[1024]{0:T(1024)S(1)}, f32[1024]{0:T(1024)}, u32[]{:S(2)}) copy-start(f32[1024]{0:T(1024)} %get-tuple-element.701) | copy-start | bytes 12292
  1059.8 40.1 %copy-start.201 = (f32[1024]{0:T(1024)S(1)}, f32[1024]{0:T(1024)}, u32[]{:S(2)}) copy-start(f32[1024]{0:T(1024)} %get-tuple-element.702) | copy-start | bytes 12292
  1059.8 111.1 %copy-start.248 = (f32[128]{0:T(128)S(1)}, f32[128]{0:T(128)}, u32[]{:S(2)}) copy-start(f32[128]{0:T(128)} %get-tuple-element.728) | copy-start | bytes 1540
  1059.8 111.1 %copy-start.249 = (f32[128]{0:T(128)S(1)}, f32[128]{0:T(128)}, u32[]{:S(2)}) copy-start(f32[128]{0:T(128)} %get-tuple-element.727) | copy-start | bytes 1540
  1059.8 111.1 %copy-start.254 = (f32[128]{0:T(128)S(1)}, f32[128]{0:T(128)}, u32[]{:S(2)}) copy-start(f32[128]{0:T(128)} %get-tuple-element.719) | copy-start | bytes 1540
  1059.8 111.1 %copy-start.255 = (f32[128]{0:T(128)S(1)}, f32[128]{0:T(128)}, u32[]{:S(2)}) copy-start(f32[128]{0:T(128)} %get-tuple-element.720) | copy-start | bytes 1540
  1059.9 111.1 %copy-start.256 = (f32[128]{0:T(128)S(1)}, f32[128]{0:T(128)}, u32[]{:S(2)}) copy-start(f32[128]{0:T(128)} %get-tuple-element.721) | copy-start | bytes 1540
  1059.9 111.1 %copy-start.257 = (f32[128]{0:T(128)S(1)}, f32[128]{0:T(128)}, u32[]{:S(2)}) copy-start(f32[128]{0:T(128)} %get-tuple-element.722) | copy-start | bytes 1540
  1059.9 115.4 %copy-start.110 = (f32[1,1024]{1,0:T(1,128)S(1)}, f32[1,1024]{1,0:T(1,128)}, u32[]{:S(2)}) copy-start(f32[1,1024]{1,0:T(1,128)} %copy-done.108) | copy-start | bytes 12292
  1059.9 115.4 %copy-start.116 = (f32[1024]{0:T(1024)S(1)}, f32[1024]{0:T(1024)}, u32[]{:S(2)}) copy-start(f32[1024]{0:T(1024)} %copy-done.115) | copy-start | bytes 12292
  1059.9 118.6 %copy-start.194 = (f32[1024]{0:T(1024)S(1)}, f32[1024]{0:T(1024)}, u32[]{:S(2)}) copy-start(f32[1024]{0:T(1024)} %get-tuple-element.709) | copy-start | bytes 12292
  1059.9 200.2 %copy-start.156 = (f32[1,4,2,128]{3,1,2,0:T(4,128)S(1)}, f32[1,4,2,128]{3,1,2,0:T(4,128)}, u32[]{:S(2)}) copy-start(f32[1,4,2,128]{3,1,2,0:T(4,128)} %copy-done.155) | copy-start | bytes 12292
  1059.9 247.4 %all-reduce.55.cloned.1.call-start = ((), (), s32[]{:S(2)}) async-start(), calls=%async_computation.32 | async-start | bytes 6553600 | tf_op jit(solution)/shard_map/psum | solution.py:396
  (233 other events, 3066.8 us)
Sparse Core Ops, SparseCore 0:
  12.2 55.5 all-gather.24
  126.0 37.2 all-gather.26
  165.6 35.1 all-gather.28
  223.2 28.4 all-reduce.46
  253.6 54.0 all-gather.30
  363.3 37.2 all-gather.32
  402.6 35.1 all-gather.34
  488.9 35.1 all-gather.36
  561.9 7.7 reduce-scatter.30
  686.5 22.8 all-reduce.50
  712.7 29.5 all-reduce.48
  783.1 36.5 all-gather.38
  846.1 7.9 reduce-scatter.32
  860.0 35.2 reduce-scatter.28
  897.9 24.0 reduce-scatter.20
  925.1 35.1 reduce-scatter.26
  962.9 24.0 reduce-scatter.18
  990.1 52.7 reduce-scatter.16
  1046.4 52.6 reduce-scatter.14
  1102.5 22.4 reduce-scatter.24
  1128.4 22.4 reduce-scatter.22
  1154.0 21.2 all-reduce.52
  1178.1 129.2 all-reduce.54
where the time goes:
time: 1330 us; the launch traced here: 1320 us
  matrix products  387 us (29%)
  waiting for transfers between devices  287 us (22%)
  local copies, waits for them, and re-layouts  229 us (17%)
  other arithmetic  210 us (16%)
  blocking collectives  170 us (13%)
  starting transfers between devices  22.6 us (2%)
  between operations  17.9 us (1%)
    dot_general x6, matrix products, state_local(): jnp.einsum('scdh,sdhpn->schpn', carry_in, fresh_state, precision=highest_...  89.7 us
    psum x1, blocking collectives, body(): lax.psum((stacked_small[0], stacked_small[1], stacked_small[2], stacked_s...  81.5 us
    all_gather x2, waiting for transfers between devices, fetch(): lax.all_gather(part_zx, 'ctx', axis=0, tiled=True)  60.8 us
    dot_general x4, matrix products, state_local(): jnp.einsum('sch,schpn->shpn', jnp.exp(total_log[:, None, :] - after_each)...  56.2 us
    reduce_scatter x2, waiting for transfers between devices, body(): lax.psum_scatter(grad_dt.astype(jnp.bfloat16), 'ctx', scatter_dimension=0...  51 us
    unnamed x548, local copies, waits for them, and re-layouts  44 us
    psum x1, waiting for transfers between devices, body(): lax.psum(shards[0].astype(jnp.bfloat16), 'dp').astype(jnp.float32)  42.5 us
    reduce_scatter x2, waiting for transfers between devices, body(): lax.psum_scatter(grad_zx.astype(jnp.bfloat16), 'ctx', scatter_dimension=0...  39 us
  transfers between devices with their start and end apart: 31, of which 15 were waited for; matrix products, arithmetic and copies ran while one was open for 42% of the time, Pallas kernels for 0%

commit v1 on v0

v1 whole, which is shorter than its diff:
```python
import jax
import jax.numpy as jnp
from jax import lax
from jax.experimental import pallas as pl
from jax.experimental.pallas import tpu as pltpu
from jax.sharding import PartitionSpec as P

HEAD_DIM = 64
STATE = 128
KCONV = 4
LAYERS = 2
DI = 2048
PAIR = 128
WIDE = 256
SPAN = 256
HALO = 8

epsilon = 1e-05
highest_precision = lax.Precision.HIGHEST
f32 = jnp.float32
bf16 = jnp.bfloat16


def along(shard, by):
    count = lax.axis_size("ctx")
    pairs = [(i, i + by) for i in range(count) if 0 <= i + by < count]
    return lax.ppermute(shard, "ctx", pairs)


def swap(shard):
    return lax.ppermute(shard, "tensor", [(0, 1), (1, 0)])


def chain(log_total, state, way):
    count = lax.axis_size("ctx")
    sent = state.astype(bf16)
    logs = jnp.zeros_like(log_total)
    total = jnp.zeros(state.shape, f32)
    for hop in range(1, count):
        part = along(sent, way * hop).astype(f32)
        factor = jnp.repeat(jnp.exp(logs), HEAD_DIM, axis=1)[:, :, None]
        total = total + factor * part
        if hop < count - 1:
            logs = logs + along(log_total, way * hop)
    return total


def prenorm(stream, gain):
    inv_rms = lax.rsqrt(jnp.mean(stream * stream, axis=-1, keepdims=True) + epsilon)
    return stream * inv_rms * gain


def conv_act(padded, kernel, offset):
    length = padded.shape[1] - KCONV + 1
    summed = offset
    for tap_index in range(KCONV):
        summed = summed + kernel[tap_index] * padded[:, tap_index : tap_index + length]
    return jax.nn.silu(summed)


def dot(a, b, over):
    return lax.dot_general(a, b, (((over[0],), (over[1],)), ((), ())), preferred_element_type=f32)


def selector(place, heads, width):
    row = lax.broadcasted_iota(jnp.int32, (heads, width), 0)
    lane = lax.broadcasted_iota(jnp.int32, (heads, width), 1)
    head = place * (width // HEAD_DIM) + lax.shift_right_logical(lane, 6)
    return jnp.where(row == head, 1.0, 0.0).astype(bf16)


def spread(values, select, terms):
    rest, total = values, None
    for term in range(terms):
        piece = rest.astype(bf16)
        part = dot(piece, select, (1, 0))
        total = part if total is None else total + part
        rest = rest - piece.astype(f32)
    return total


def gathered(values, select):
    high = values.astype(bf16)
    low = (values - high.astype(f32)).astype(bf16)
    return dot(high, select, (1, 1)) + dot(low, select, (1, 1))


def head_lanes(values, member):
    lane = lax.broadcasted_iota(jnp.int32, values.shape, 1)
    return jnp.where(lax.shift_right_logical(lane, 6) == member, values, jnp.zeros_like(values))


def decay_of(wide_log, row_log, member, start):
    stop = start + SPAN
    column = wide_log[start:stop, member * HEAD_DIM : member * HEAD_DIM + 1]
    differ = column - row_log[member : member + 1, :stop]
    token = lax.broadcasted_iota(jnp.int32, differ.shape, 0) + start
    other = lax.broadcasted_iota(jnp.int32, differ.shape, 1)
    return jnp.where(other <= token, jnp.exp(differ), 0.0)


def sigmoid(v):
    return 1.0 / (1.0 + jnp.exp(-v))


def convolve(pad_ref, values, rim, taps, offset):
    length = values.shape[0]
    pad_ref[0:HALO, :] = rim
    pad_ref[HALO : HALO + length, :] = values
    summed = offset
    for tap in range(KCONV):
        begin = HALO - KCONV + 1 + tap
        summed = summed + taps[tap : tap + 1] * pad_ref[begin : begin + length, :]
    return summed


def state_kernel(inner_ref, rim_ref, taps_ref, bias_ref, log_ref, step_ref, keys_ref, x_ref, state_ref, pad_ref):
    select = selector(pl.program_id(1), log_ref.shape[2], PAIR)
    length = inner_ref.shape[0]
    pre = convolve(pad_ref, inner_ref[...].astype(f32), rim_ref[0], taps_ref[...], bias_ref[...])
    x = (pre * sigmoid(pre)).astype(bf16)
    x_ref[...] = x
    wide_log = spread(log_ref[0], select, 3)
    wide_step = spread(step_ref[0], select, 2)
    weighted = x.astype(f32) * wide_step * jnp.exp(wide_log[length - 1 :] - wide_log)
    state_ref[0] = dot(weighted.astype(bf16), keys_ref[...], (0, 0)).astype(bf16)


def output_kernel(x_ref, gate_ref, keys_ref, queries_ref, log_ref, row_ref, step_ref, state_ref, skip_ref, gain_ref, ssd_ref, out_ref, square_ref, score_ref):
    place = pl.program_id(1)
    select = selector(place, log_ref.shape[2], PAIR)
    length = x_ref.shape[0]

    @pl.when(place == 0)
    def _():
        score_ref[...] = dot(queries_ref[...], keys_ref[...], (1, 1))
        square_ref[...] = jnp.zeros_like(square_ref)

    x = x_ref[...].astype(f32)
    wide_log = spread(log_ref[0], select, 3)
    wide_step = spread(step_ref[0], select, 2)
    scaled = (x * wide_step).astype(bf16)
    split = [head_lanes(scaled, member) for member in range(2)]
    rows = []
    for start in range(0, length, SPAN):
        stop = start + SPAN
        total = None
        for member in range(2):
            decay = decay_of(wide_log, row_ref[0, 0], member, start)
            mixing = (score_ref[start:stop, :stop] * decay).astype(bf16)
            part = dot(mixing, split[member][:stop], (1, 0))
            total = part if total is None else total + part
        rows.append(total)
    within = jnp.concatenate(rows, axis=0)
    carried = jnp.exp(wide_log) * dot(queries_ref[...], state_ref[0], (1, 1))
    ssd = within + carried + skip_ref[...] * x
    gate = gate_ref[...].astype(f32)
    gated = ssd * gate * sigmoid(gate)
    ssd_ref[...] = ssd.astype(bf16)
    out_ref[...] = (gated * gain_ref[...]).astype(bf16)
    square_ref[...] += gated * gated


def gate_kernel(grad_ref, weight_ref, gate_ref, ssd_ref, gain_ref, inv_ref, cross_ref, log_ref, queries_ref, d_ssd_ref, d_gate_ref, norm_ref, state_ref):
    select = selector(pl.program_id(1), log_ref.shape[2], WIDE)
    d_out = dot(grad_ref[...], weight_ref[...], (1, 0))
    gate = gate_ref[...].astype(f32)
    ssd = ssd_ref[...].astype(f32)
    sig = sigmoid(gate)
    silu = gate * sig
    gated = ssd * silu
    inv = inv_ref[...]
    norm_ref[0] = jnp.sum(d_out * gated * inv, axis=0, keepdims=True)
    d_gated = inv * (d_out * gain_ref[...]) - gated * cross_ref[...]
    d_gate_ref[...] = (d_gated * ssd * sig * (1.0 + gate * (1.0 - sig))).astype(bf16)
    d_ssd = (d_gated * silu).astype(bf16)
    d_ssd_ref[...] = d_ssd
    wide_log = spread(log_ref[0], select, 3)
    weighted = (d_ssd.astype(f32) * jnp.exp(wide_log)).astype(bf16)
    state_ref[0] = dot(weighted, queries_ref[...], (0, 0)).astype(bf16)


def grad_kernel(
    x_ref, inner_ref, rim_ref, taps_ref, bias_ref, keys_ref, queries_ref, log_ref, row_ref, step_ref, state_ref, lam_ref, skip_ref, d_ssd_ref,
    d_inner_ref, d_rim_ref, d_taps_ref, d_bias_ref, d_skip_ref, d_keys_ref, d_queries_ref, d_log_ref, d_end_ref, d_step_ref,
    score_ref, d_score_ref, pad_ref, tail_ref, d_scaled_ref,
):
    place = pl.program_id(1)
    select = selector(place, log_ref.shape[2], PAIR)
    length = x_ref.shape[0]
    keys, queries = keys_ref[...], queries_ref[...]

    @pl.when(place == 0)
    def _():
        score_ref[...] = dot(queries, keys, (1, 1))
        for ref in (d_score_ref, d_keys_ref, d_queries_ref, d_log_ref, d_end_ref, d_step_ref):
            ref[...] = jnp.zeros_like(ref)

    x = x_ref[...].astype(f32)
    d_ssd = d_ssd_ref[...]
    d_ssd_f = d_ssd.astype(f32)
    wide_log = spread(log_ref[0], select, 3)
    wide_step = spread(step_ref[0], select, 2)
    scaled = (x * wide_step).astype(bf16)
    scaled_f = scaled.astype(f32)
    split = [head_lanes(scaled, member) for member in range(2)]
    d_split = [head_lanes(d_ssd, member) for member in range(2)]
    d_scaled_ref[...] = jnp.zeros_like(d_scaled_ref)
    rows = []
    for start in range(0, length, SPAN):
        stop = start + SPAN
        total, back, d_score = None, None, None
        for member in range(2):
            decay = decay_of(wide_log, row_ref[0, 0], member, start)
            mixing = (score_ref[start:stop, :stop] * decay).astype(bf16)
            part = dot(mixing, split[member][:stop], (1, 0))
            grad = dot(mixing, d_split[member][start:stop], (0, 0))
            d_part = dot(d_ssd[start:stop], split[member][:stop], (1, 1)) * decay
            total = part if total is None else total + part
            back = grad if back is None else back + grad
            d_score = d_part if d_score is None else d_score + d_part
        rows.append(total)
        d_scaled_ref[:stop, :] += back
        d_score_ref[start:stop, :stop] += d_score
    grown = jnp.exp(wide_log)
    fading = jnp.exp(wide_log[length - 1 :] - wide_log)
    read = jnp.concatenate(rows, axis=0) + grown * dot(queries, state_ref[0], (1, 1))
    d_within = d_scaled_ref[...]
    d_state = fading * dot(keys, lam_ref[0], (1, 1))
    d_scaled = d_within + d_state
    d_log_ref[0] += gathered(d_ssd_f * read - scaled_f * d_within, select)
    d_end_ref[0] += gathered(scaled_f * d_state, select)
    d_step_ref[0] += gathered(x * d_scaled, select)
    d_skip_ref[0] = jnp.sum(d_ssd_f * x, axis=0, keepdims=True)
    d_keys_ref[...] += dot((scaled_f * fading).astype(bf16), lam_ref[0], (1, 0))
    d_queries_ref[...] += dot((d_ssd_f * grown).astype(bf16), state_ref[0], (1, 0))

    taps = taps_ref[...]
    pre = convolve(pad_ref, inner_ref[...].astype(f32), rim_ref[0], taps, bias_ref[...])
    sig = sigmoid(pre)
    d_pre = (wide_step * d_scaled + skip_ref[...] * d_ssd_f) * sig * (1.0 + pre * (1.0 - sig))
    d_bias_ref[0] = jnp.sum(d_pre, axis=0, keepdims=True)
    tail_ref[0:HALO, :] = jnp.zeros((HALO, PAIR), f32)
    tail_ref[HALO : HALO + length, :] = d_pre
    tail_ref[HALO + length :, :] = jnp.zeros((HALO, PAIR), f32)
    inner = None
    rim = None
    for tap in range(KCONV):
        begin = HALO - KCONV + 1 + tap
        d_taps_ref[0, tap : tap + 1, :] = jnp.sum(d_pre * pad_ref[begin : begin + length, :], axis=0, keepdims=True)
        ahead = KCONV - 1 - tap
        part = taps[tap : tap + 1] * tail_ref[HALO + ahead : HALO + ahead + length, :]
        edge = taps[tap : tap + 1] * tail_ref[ahead : ahead + HALO, :]
        inner = part if inner is None else inner + part
        rim = edge if rim is None else rim + edge
    d_inner_ref[...] = inner.astype(bf16)
    d_rim_ref[0] = rim

    @pl.when(place == pl.num_programs(1) - 1)
    def _():
        d_scores = d_score_ref[...].astype(bf16)
        d_queries_ref[...] += dot(d_scores, keys, (1, 0))
        d_keys_ref[...] += dot(d_scores, queries, (0, 0))


params = pltpu.CompilerParams(vmem_limit_bytes=48 * 1024 * 1024)


def body(
    hidden,
    out_grad,
    pre_gain,
    gate_inner_weight,
    state_maps_weight,
    step_size_weight,
    conv_x,
    bias_x,
    conv_bc,
    bias_bc,
    dt_bias,
    a_log,
    d_skip,
    norm_gain,
    output_weight,
):
    seqs, length, width = hidden.shape
    rows = seqs * length
    depth = gate_inner_weight.shape[1]
    inner = gate_inner_weight.shape[3]
    heads = inner // HEAD_DIM
    pairs = inner // PAIR
    maps = state_maps_weight.shape[2]
    first_maps, first_dt = 2 * inner, 2 * inner + maps
    columns = first_dt + 128
    core = lax.axis_index("tensor")
    lower = (jnp.arange(length)[:, None] >= jnp.arange(length)[None, :]).astype(f32)
    strict = (jnp.arange(length)[:, None] > jnp.arange(length)[None, :]).astype(f32)

    def run_sum(tri, values, order):
        return jnp.einsum(order, tri, values, precision=highest_precision)

    def cols(offset=0, wide=PAIR):
        return pl.BlockSpec((length, wide), lambda s, j: (s, j + offset))

    per_seq = pl.BlockSpec((length, STATE), lambda s, j: (s, 0))
    head_spec = pl.BlockSpec((1, length, heads), lambda s, j: (s, 0, 0))
    row_spec = pl.BlockSpec((1, 1, 2, length), lambda s, j: (s, j, 0, 0))
    state_spec = pl.BlockSpec((1, PAIR, STATE), lambda s, j: (s, j, 0))
    rim_spec = pl.BlockSpec((1, HALO, PAIR), lambda s, j: (s, 0, j))
    taps_spec = pl.BlockSpec((KCONV, PAIR), lambda s, j: (0, j))
    lane_spec = pl.BlockSpec((1, PAIR), lambda s, j: (0, j))
    sum_spec = pl.BlockSpec((1, 1, PAIR), lambda s, j: (s, 0, j))

    def shape(dims, kind):
        return jax.ShapeDtypeStruct(dims, kind)

    def shards(l):
        into = jnp.concatenate(
            [
                gate_inner_weight[l].reshape(depth, 2 * inner),
                state_maps_weight[l],
                jnp.pad(step_size_weight[l], ((0, 0), (0, 128 - heads))),
            ],
            axis=1,
        )
        return into, output_weight[l].T

    def gather(v):
        return lax.all_gather(v, "ctx", axis=0, tiled=True)

    stream = hidden.astype(f32).reshape(rows, width)
    kept = []
    for l in range(LAYERS):
        into, out_t = shards(l)
        if l > 0:
            kept[l - 1][0], into = lax.optimization_barrier((kept[l - 1][0], into))
        full_in = gather(into)
        full_in, out_t = lax.optimization_barrier((full_in, out_t))
        full_out = gather(out_t)
        normed_f, norm_pull = jax.vjp(prenorm, stream, pre_gain[l])
        normed = normed_f.astype(bf16)
        proj = jnp.dot(normed, full_in, preferred_element_type=f32).astype(bf16)
        rims = along(proj.reshape(seqs, length, columns)[:, length - KCONV + 1 :, inner:first_dt], 1).astype(f32)
        rim_x = jnp.pad(rims[:, :, :inner], ((0, 0), (HALO - KCONV + 1, 0), (0, 0)))
        bc = proj[:, first_maps:first_dt].astype(f32).reshape(seqs, length, maps)
        padded_bc = jnp.concatenate([rims[:, :, inner:], bc], axis=1)
        act_bc, pull_bc = jax.vjp(conv_act, padded_bc, conv_bc[l], bias_bc[l])
        own = act_bc.astype(bf16).reshape(rows, maps)
        other = swap(own)
        keys = jnp.where(core == 0, own, other)
        queries = jnp.where(core == 0, other, own)
        raw = proj[:, first_dt : first_dt + heads].astype(f32).reshape(seqs, length, heads)
        step = jax.nn.softplus(raw + dt_bias[l])
        rate = jnp.exp(a_log[l])
        log = run_sum(lower, -rate * step, "tu,suh->sth")
        row_log = jnp.swapaxes(log, 1, 2).reshape(seqs, pairs, 2, length)
        log_total = log[:, -1]
        taps, offset = conv_x[l], bias_x[l][None]
        x, state = pl.pallas_call(
            state_kernel,
            grid=(seqs, pairs),
            in_specs=[cols(pairs), rim_spec, taps_spec, lane_spec, head_spec, head_spec, per_seq],
            out_specs=[cols(), state_spec],
            out_shape=[shape((rows, inner), bf16), shape((seqs, inner, STATE), bf16)],
            scratch_shapes=[pltpu.VMEM((HALO + length, PAIR), f32)],
            compiler_params=params,
        )(proj, rim_x, taps, offset, log, step, keys)
        state_in = chain(log_total, state, 1).astype(bf16)
        skip = jnp.repeat(d_skip[l], HEAD_DIM)[None]
        gain = norm_gain[l][None]
        ssd, gated, square = pl.pallas_call(
            output_kernel,
            grid=(seqs, pairs),
            in_specs=[cols(), cols(), per_seq, per_seq, head_spec, row_spec, head_spec, state_spec, lane_spec, lane_spec],
            out_specs=[cols(), cols(), per_seq],
            out_shape=[shape((rows, inner), bf16), shape((rows, inner), bf16), shape((rows, PAIR), f32)],
            scratch_shapes=[pltpu.VMEM((length, length), f32)],
            compiler_params=params,
        )(x, proj, keys, queries, log, row_log, step, state_in, skip, gain)
        square = jnp.sum(square, axis=1)
        square = square + swap(square)
        inv_rms = lax.rsqrt(square / DI + epsilon)[:, None]
        part = dot(gated, full_out, (1, 1)).astype(bf16)
        mixed = part.astype(f32) + swap(part).astype(f32)
        kept.append(
            [full_in, full_out, norm_pull, normed, proj, rim_x, pull_bc, keys, queries, raw, step, rate, log, row_log,
             log_total, x, state_in, skip, gain, ssd, gated, inv_rms, mixed]
        )
        stream = stream + mixed * inv_rms
    output = stream.reshape(seqs, length, width)

    grad = out_grad.astype(f32).reshape(rows, width)
    sums = [None] * LAYERS
    small = [None] * LAYERS
    for l in reversed(range(LAYERS)):
        (full_in, full_out, norm_pull, normed, proj, rim_x, pull_bc, keys, queries, raw, step, rate, log, row_log,
         log_total, x, state_in, skip, gain, ssd, gated, inv_rms, mixed) = kept[l]
        taps, offset = conv_x[l], bias_x[l][None]
        grad_b = grad.astype(bf16)
        cross = jnp.sum(grad_b.astype(f32) * mixed, axis=1, keepdims=True) * (inv_rms * inv_rms * inv_rms) / DI
        blocks = inner // WIDE
        wide_lane = pl.BlockSpec((1, WIDE), lambda s, j: (0, j))
        token_spec = pl.BlockSpec((length, 1), lambda s, j: (s, 0))
        d_ssd, d_gate, grad_norm, d_state = pl.pallas_call(
            gate_kernel,
            grid=(seqs, blocks),
            in_specs=[
                pl.BlockSpec((length, width), lambda s, j: (s, 0)),
                pl.BlockSpec((width, WIDE), lambda s, j: (0, j)),
                cols(0, WIDE), cols(0, WIDE), wide_lane, token_spec, token_spec, head_spec, per_seq,
            ],
            out_specs=[
                cols(0, WIDE), cols(0, WIDE),
                pl.BlockSpec((1, 1, WIDE), lambda s, j: (s, 0, j)),
                pl.BlockSpec((1, WIDE, STATE), lambda s, j: (s, j, 0)),
            ],
            out_shape=[
                shape((rows, inner), bf16), shape((rows, inner), bf16),
                shape((seqs, 1, inner), f32), shape((seqs, inner, STATE), bf16),
            ],
            compiler_params=params,
        )(grad_b, full_out, proj, ssd, gain, inv_rms, cross, log, queries)
        lam = chain(log_total, d_state, -1)
        through = jnp.sum((lam * state_in.astype(f32)).reshape(seqs, heads, HEAD_DIM * STATE), axis=2) * jnp.exp(log_total)
        grad_out = dot((grad_b.astype(f32) * inv_rms).astype(bf16), gated, (0, 0)).astype(bf16)
        out_shard = lax.psum_scatter(grad_out, "ctx", scatter_dimension=0, tiled=True)
        (d_inner, d_rim, d_taps, d_offset, skip_sum, d_keys, d_queries, d_log, d_end, d_step) = pl.pallas_call(
            grad_kernel,
            grid=(seqs, pairs),
            in_specs=[
                cols(), cols(pairs), rim_spec, taps_spec, lane_spec, per_seq, per_seq, head_spec, row_spec, head_spec,
                state_spec, state_spec, lane_spec, cols(),
            ],
            out_specs=[
                cols(), rim_spec, pl.BlockSpec((1, KCONV, PAIR), lambda s, j: (s, 0, j)), sum_spec, sum_spec,
                per_seq, per_seq, head_spec, head_spec, head_spec,
            ],
            out_shape=[
                shape((rows, inner), bf16), shape((seqs, HALO, inner), f32), shape((seqs, KCONV, inner), f32),
                shape((seqs, 1, inner), f32), shape((seqs, 1, inner), f32),
                shape((rows, STATE), f32), shape((rows, STATE), f32),
            ]
            + [shape((seqs, length, heads), f32)] * 3,
            scratch_shapes=[
                pltpu.VMEM((length, length), f32),
                pltpu.VMEM((length, length), f32),
                pltpu.VMEM((HALO + length, PAIR), f32),
                pltpu.VMEM((2 * HALO + length, PAIR), f32),
                pltpu.VMEM((length, PAIR), f32),
            ],
            compiler_params=params,
        )(x, proj, rim_x, taps, offset, keys, queries, log, row_log, step, state_in, lam.astype(bf16), skip, d_ssd)
        theirs = swap(jnp.where(core == 0, d_queries, d_keys).astype(bf16)).astype(f32)
        d_own = jnp.where(core == 0, d_keys, d_queries) + theirs
        d_pad_bc, grad_conv_bc, grad_bias_bc = pull_bc(d_own.reshape(seqs, length, maps))
        edge = along(
            jnp.concatenate([d_rim[:, HALO - KCONV + 1 :], d_pad_bc[:, : KCONV - 1]], axis=2), -1
        )
        d_inner = d_inner.reshape(seqs, length, inner)
        d_tail = (d_inner[:, length - KCONV + 1 :].astype(f32) + edge[:, :, :inner]).astype(bf16)
        d_inner = lax.dynamic_update_slice(d_inner, d_tail, (0, length - KCONV + 1, 0)).reshape(rows, inner)
        d_bc = d_pad_bc[:, KCONV - 1 :].at[:, length - KCONV + 1 :].add(edge[:, :, inner:])
        d_decay = (
            run_sum(lower, d_log, "ut,suh->sth")
            + run_sum(strict, d_end, "tu,suh->sth")
            + through[:, None, :]
        )
        grad_rate = jnp.sum(d_decay * (-rate * step), axis=(0, 1))
        d_raw = (d_step - rate * d_decay) * jax.nn.sigmoid(raw + dt_bias[l])
        grad_dt = jnp.sum(d_raw, axis=(0, 1))
        d_proj = jnp.concatenate(
            [
                d_gate,
                d_inner,
                d_bc.reshape(rows, maps).astype(bf16),
                jnp.pad(d_raw.reshape(rows, heads).astype(bf16), ((0, 0), (0, 128 - heads))),
            ],
            axis=1,
        )
        part = dot(d_proj, full_in, (1, 1)).astype(bf16)
        d_normed = part.astype(f32) + swap(part).astype(f32)
        if l + 1 < LAYERS:
            normed, sums[l + 1] = lax.optimization_barrier((normed, sums[l + 1]))
        grad_in = dot(normed, d_proj, (0, 0)).astype(bf16)
        in_shard = lax.psum_scatter(grad_in, "ctx", scatter_dimension=0, tiled=True)
        d_stream, grad_pre = norm_pull(d_normed)
        grad = grad + d_stream
        sums[l] = (lax.psum(in_shard, "dp"), lax.psum(out_shard, "dp"))
        small[l] = (
            grad_pre,
            jnp.sum(d_taps, axis=0),
            jnp.sum(d_offset, axis=(0, 1)),
            grad_conv_bc,
            grad_bias_bc,
            grad_dt,
            grad_rate,
            jnp.sum(skip_sum.reshape(seqs, heads, HEAD_DIM), axis=(0, 2)),
            jnp.sum(grad_norm, axis=(0, 1)),
        )
    big = [
        (
            in_sum[:, :first_maps].reshape(depth, 2, inner).astype(f32),
            in_sum[:, first_maps:first_dt].astype(f32),
            in_sum[:, first_dt : first_dt + heads].astype(f32),
            out_sum.T.astype(f32),
        )
        for in_sum, out_sum in sums
    ]
    flat = jnp.concatenate([v.reshape(-1) for l in range(LAYERS) for v in small[l]])
    flat = lax.psum(flat, ("dp", "ctx"))
    summed = []
    at = 0
    for l in range(LAYERS):
        row = []
        for v in small[l]:
            row.append(flat[at : at + v.size].reshape(v.shape))
            at += v.size
        summed.append(row)
    s = [jnp.stack([summed[l][m] for l in range(LAYERS)]) for m in range(9)]
    b = [jnp.stack([big[l][m] for l in range(LAYERS)]) for m in range(4)]
    grad_hidden = grad.reshape(seqs, length, width)
    return (output, grad_hidden, s[0], b[0], b[1], b[2], s[1], s[2], s[3], s[4], s[5], s[6], s[7], s[8], b[3])


def solution(mesh):
    return jax.shard_map(
        body,
        mesh=mesh,
        in_specs=(
            P("dp", "ctx", None),
            P("dp", "ctx", None),
            P(),
            P(None, "ctx", None, "tensor"),
            P(None, "ctx", "tensor"),
            P(None, "ctx", "tensor"),
            P(None, None, "tensor"),
            P(None, "tensor"),
            P(None, None, "tensor"),
            P(None, "tensor"),
            P(None, "tensor"),
            P(None, "tensor"),
            P(None, "tensor"),
            P(None, "tensor"),
            P(None, "tensor", "ctx"),
        ),
        out_specs=(
            P("dp", "ctx", None),
            P("dp", "ctx", None),
            P(),
            P(None, "ctx", None, "tensor"),
            P(None, "ctx", "tensor"),
            P(None, "ctx", "tensor"),
            P(None, None, "tensor"),
            P(None, "tensor"),
            P(None, None, "tensor"),
            P(None, "tensor"),
            P(None, "tensor"),
            P(None, "tensor"),
            P(None, "tensor"),
            P(None, "tensor"),
            P(None, "tensor", "ctx"),
        ),
        check_vma=False,
    )
```

time: 1330 us -> 832 us (0.63)
  matrix products: 387 us -> 84 us
  Pallas kernels: 0 us -> 166 us
  local copies, waits for them, and re-layouts: 229 us -> 71.9 us
  other arithmetic: 210 us -> 91.6 us
  blocking collectives: 170 us -> 75.3 us
  starting transfers between devices: 22.6 us -> 49.8 us
  waiting for transfers between devices: 287 us -> 266 us
    dot_general x58 -> x16, matrix products: 387 us -> 84 us  [the longest x8 59.4 us: dot(): lax.dot_general(a, b, (((over[0],), (over[1],)), ((), ())), preferred_ele...]
    pallas_call x0 -> x8, Pallas kernels: none -> 166 us  [the longest x2 77.4 us: body(): pl.pallas_call(grad_kernel, grid=(seqs, pairs), in_specs=[cols(), cols(pa...]
    ppermute x8 -> x34, waiting for transfers between devices: 24.9 us -> 118 us  [the longest x24 112 us: along(): return lax.ppermute(shard, 'ctx', pairs)]
    reshape x16 -> x2, local copies, waits for them, and re-layouts: 73 us -> 0.08 us  [body(): row_log = jnp.swapaxes(log, 1, 2).reshape(seqs, pairs, 2, length)]
    all_gather x8 -> x0, blocking collectives: 58.8 us -> none  [the longest x2 20 us: prefix(): lax.all_gather(part.astype(kind), axis)]
    reduce_scatter x8 -> x4, waiting for transfers between devices: 90.1 us -> 34.6 us  [the longest x2 34.6 us: body(): in_shard = lax.psum_scatter(grad_in, 'ctx', scatter_dimension=0, tiled=True)]
    convert_element_type x12 -> x2, local copies, waits for them, and re-layouts: 42.9 us -> 3.16 us  [body(): in_sum[:, :first_maps].reshape(depth, 2, inner).astype(f32)]
    psum x5 -> x2, waiting for transfers between devices: 94.9 us -> 56.5 us  [body(): sums[l] = (lax.psum(in_shard, 'dp'), lax.psum(out_shard, 'dp'))]
  transfers between devices with their start and end apart: 31 -> 44, of which waited for: 15 -> 19; matrix products, arithmetic and copies ran while one was open for 42% -> 23% of each run, Pallas kernels for 0% -> 19%
where the time goes in v1:
time: 832 us; the launch traced here: 821 us
  waiting for transfers between devices  266 us (32%)
  Pallas kernels  166 us (20%)
  other arithmetic  91.6 us (11%)
  matrix products  84 us (10%)
  blocking collectives  75.3 us (9%)
  local copies, waits for them, and re-layouts  71.9 us (9%)
  starting transfers between devices  49.8 us (6%)
  between operations  16.7 us (2%)
    ppermute x24, waiting for transfers between devices, along(): return lax.ppermute(shard, 'ctx', pairs)  112 us
    pallas_call x2, Pallas kernels, body(): pl.pallas_call(grad_kernel, grid=(seqs, pairs), in_specs=[cols(), cols(pa...  77.4 us
    psum x1, blocking collectives, body(): flat = lax.psum(flat, ('dp', 'ctx'))  75.3 us
    dot_general x8, matrix products, dot(): lax.dot_general(a, b, (((over[0],), (over[1],)), ((), ())), preferred_ele...  59.4 us
    all_gather x4, waiting for transfers between devices, gather(): return lax.all_gather(v, 'ctx', axis=0, tiled=True)  56.8 us
    psum x2, waiting for transfers between devices, body(): sums[l] = (lax.psum(in_shard, 'dp'), lax.psum(out_shard, 'dp'))  56.5 us
    ppermute x24, starting transfers between devices, along(): return lax.ppermute(shard, 'ctx', pairs)  47.4 us
    pallas_call x2, Pallas kernels, body(): pl.pallas_call(output_kernel, grid=(seqs, pairs), in_specs=[cols(), cols(...  35.8 us
  transfers between devices with their start and end apart: 44, of which 19 were waited for; matrix products, arithmetic and copies ran while one was open for 23% of the time, Pallas kernels for 19%

profile of v1, /device:TPU:0, one launch (start us, length us, event | category | flops | bytes accessed | tf_op | source)
XLA Modules:
  0.0 821.2 jit_solution(12790631276115514708)
XLA Ops:
  9.0 3.5 fusion.108
  13.9 2.1 fusion.109
  17.0 56.8 %all-gather.5.cloned.1.call-done = bf16[1024,2304]{1,0:T(8,128)(2,1)} async-done(((bf16[256,2304]{1,0:T(8,128)(2,1)}), bf16[1024,2304]{1,0:T(8,128)(2,1)}) %all-gather.5.cloned.1.call-update) | async-done | bytes 4718608 | tf_op jit(solution)/shard_map/all_gather | solution.py:329
  79.1 2.1 fusion.11
  81.3 10.0 %convolution_convert_fusion.3.inner_ref.gate_ref = bf16[1024,2304]{1,0:T(8,128)(2,1)} fusion(bf16[1024,1024]{1,0:T(8,128)(2,1)S(1)} %fusion.11, bf16[1024,2304]{1,0:T(8,128)(2,1)} %all-gather.5.cloned.1.call-done), kind=kOutput, calls=%fused_computation.11 | convolution fusion | flops 4834197504 | bytes 11534336 | tf_op jit(solution)/shard_map/dot_general | solution.py:342
  92.2 3.4 collective-permute-start
  101.7 13.2 %shard_map.262 = (bf16[1024,1024]{1,0:T(8,128)(2,1)S(1)}, bf16[2,1024,128]{2,1,0:T(8,128)(2,1)S(1)}) custom-call(bf16[1024,2304]{1,0:T(8,128)(2,1)} %convolution_convert_fusion.3.inner_ref.gate_ref, f32[2,8,1024]{2,1,0:T(8,128)S(1)} %pad.74.rim_ref, f32[4,1024]{1,0:T(4,128)S(1)} %get-tuple-element.287.taps_ref, f32[1,1024]{1,0:T(1,128)S(1)} %get-tuple-element.293.bias_ref, ...), custom_call_target="tpu_custom_call" | custom-call | tf_op jit(solution)/shard_map/pallas_call | solution.py:359
  116.3 3.3 collective-permute-start.6
  119.6 1.8 collective-permute-start.4
  121.4 2.8 collective-permute-start.2
  126.3 2.0 collective-permute-start.3
  128.4 27.4 %collective-permute-done.5 = f32[2,16]{1,0:T(2,128)S(1)} collective-permute-done((f32[2,16]{1,0:T(2,128)S(1)}, f32[2,16]{1,0:T(2,128)S(1)}, u32[]{:S(2)}, u32[]{:S(2)}) %collective-permute-start.5) | collective-permute-done | bytes 160 | tf_op jit(solution)/shard_map/ppermute | solution.py:27
  157.8 18.0 %shard_map.263 = (bf16[1024,1024]{1,0:T(8,128)(2,1)S(1)}, bf16[1024,1024]{1,0:T(8,128)(2,1)}, f32[1024,128]{1,0:T(8,128)S(1)}) custom-call(bf16[1024,1024]{1,0:T(8,128)(2,1)} %copy-done, bf16[1024,2304]{1,0:T(8,128)(2,1)} %convolution_convert_fusion.3.inner_ref.gate_ref, bf16[1024,128]{1,0:T(8,128)(2,1)S(1)} %get-tuple-element.265.keys_ref, ...), custom_call_target="tpu_custom_call" | custom-call | tf_op jit(solution)/shard_map/pallas_call | solution.py:371
  177.1 6.0 convolution_convert_fusion.7
  184.9 2.2 collective-permute-done.8
  187.6 6.0 multiply_reduce_fusion.2
  193.8 8.5 %convolution_convert_fusion.2.inner_ref.gate_ref = bf16[1024,2304]{1,0:T(8,128)(2,1)S(1)} fusion(bf16[1024,2304]{1,0:T(8,128)(2,1)} %all-gather.9.cloned.1.call-done, f32[1024,1024]{1,0:T(8,128)} %get-tuple-element.239, f32[1024]{0:T(1024)S(1)} %bitcast.290, f32[1024]{0:T(1024)S(1)} %fusion.93), kind=kOutput, calls=%fused_computation.10 | convolution fusion | flops 4837343232 | bytes 13639680 | tf_op jit(solution)/shard_map/dot_general | solution.py:342
  202.4 4.1 collective-permute-start.9
  212.0 1.8 broadcast_select_fusion
  213.8 14.0 %shard_map.264 = (bf16[1024,1024]{1,0:T(8,128)(2,1)S(1)}, bf16[2,1024,128]{2,1,0:T(8,128)(2,1)}) custom-call(bf16[1024,2304]{1,0:T(8,128)(2,1)} %copy-done.49, f32[2,8,1024]{2,1,0:T(8,128)S(1)} %pad.76.rim_ref, f32[4,1024]{1,0:T(4,128)S(1)} %get-tuple-element.286.taps_ref, f32[1,1024]{1,0:T(1,128)S(1)} %get-tuple-element.292.bias_ref, ...), custom_call_target="tpu_custom_call" | custom-call | tf_op jit(solution)/shard_map/pallas_call | solution.py:359
  229.1 4.9 collective-permute-start.15
  234.0 2.9 collective-permute-start.13
  236.9 2.1 collective-permute-start.11
  241.1 2.0 collective-permute-start.12
  243.1 16.5 %collective-permute-done.14 = f32[2,16]{1,0:T(2,128)S(1)} collective-permute-done((f32[2,16]{1,0:T(2,128)S(1)}, f32[2,16]{1,0:T(2,128)S(1)}, u32[]{:S(2)}, u32[]{:S(2)}) %collective-permute-start.14) | collective-permute-done | bytes 160 | tf_op jit(solution)/shard_map/ppermute | solution.py:27
  261.1 1.9 add_convert_fusion.state_ref
  266.3 17.8 %shard_map.265 = (bf16[1024,1024]{1,0:T(8,128)(2,1)S(1)}, bf16[1024,1024]{1,0:T(8,128)(2,1)}, f32[1024,128]{1,0:T(8,128)S(1)}) custom-call(bf16[1024,1024]{1,0:T(8,128)(2,1)} %copy-done.1, bf16[1024,2304]{1,0:T(8,128)(2,1)} %copy-done.49, bf16[1024,128]{1,0:T(8,128)(2,1)S(1)} %copy-done.8, bf16[1024,128]{1,0:T(8,128)(2,1)S(1)} %copy-done.2, ...), custom_call_target="tpu_custom_call" | custom-call | tf_op jit(solution)/shard_map/pallas_call | solution.py:371
  286.3 6.0 convolution_convert_fusion.6
  295.5 2.3 collective-permute-done.21
  304.4 1.8 reduce_sum.397
  306.3 3.7 fusion.6
  317.8 12.6 %shard_map.266 = (bf16[1024,1024]{1,0:T(8,128)(2,1)S(1)}, bf16[1024,1024]{1,0:T(8,128)(2,1)}, f32[2,1,1024]{2,1,0:T(1,128)S(1)}, bf16[2,1024,128]{2,1,0:T(8,128)(2,1)}) custom-call(bf16[1024,1024]{1,0:T(8,128)(2,1)} %bitcast.266, bf16[1024,1024]{1,0:T(8,128)(2,1)} %all-gather.11.cloned.1.call-done.weight_ref, bf16[1024,2304]{1,0:T(8,128)(2,1)} %copy-done.49, ...), custom_call_target="tpu_custom_call" | custom-call | tf_op jit(solution)/shard_map/pallas_call | solution.py:404
  336.3 3.9 fusion.28
  340.7 9.6 %collective-permute-done.22 = bf16[2,1024,128]{2,1,0:T(8,128)(2,1)} collective-permute-done((bf16[2,1024,128]{2,1,0:T(8,128)(2,1)}, bf16[2,1024,128]{2,1,0:T(8,128)(2,1)}, u32[]{:S(2)}, u32[]{:S(2)}) %collective-permute-start.22) | collective-permute-done | bytes 524320 | tf_op jit(solution)/shard_map/ppermute | solution.py:27
  350.2 17.9 %collective-permute-done.20 = bf16[2,1024,128]{2,1,0:T(8,128)(2,1)} collective-permute-done((bf16[2,1024,128]{2,1,0:T(8,128)(2,1)}, bf16[2,1024,128]{2,1,0:T(8,128)(2,1)}, u32[]{:S(2)}, u32[]{:S(2)}) %collective-permute-start.20) | collective-permute-done | bytes 524320 | tf_op jit(solution)/shard_map/ppermute | solution.py:27
  368.2 3.5 multiply_reduce_fusion.4
  380.3 38.7 %shard_map.267 = (bf16[1024,1024]{1,0:T(8,128)(2,1)}, f32[2,8,1024]{2,1,0:T(8,128)S(1)}, f32[2,4,1024]{2,1,0:T(4,128)S(1)}, f32[2,1,1024]{2,1,0:T(1,128)S(1)}, f...) custom-call(bf16[1024,1024]{1,0:T(8,128)(2,1)} %copy-done.1, ...), custom_call_target="tpu_custom_call" | custom-call | tf_op jit(solution)/shard_map/pallas_call | solution.py:427
  423.7 2.9 fusion.101
  426.6 2.3 multiply_reduce_fusion.7
  432.1 6.0 collective-permute-done.24
  442.9 11.0 %convolution_convert_fusion.1 = bf16[1024,2304]{1,0:T(8,128)(2,1)} fusion(bf16[1024,16]{1,0:T(8,128)(2,1)} %bitcast.288, bf16[1024,128]{1,0:T(8,128)(2,1)} %bitcast.283, bf16[1024,1024]{1,0:T(8,128)(2,1)} %bitcast.340, bf16[1024,1024]{1,0:T(8,128)(2,1)} %get-tuple-element.100, f32[1024,1024]{1,0:T(8,128)} %get-tuple-element.239, f32[1024]{0:T(1024)S(1)} %bitcast.291, ...), kind=kOutput, calls=%fused_computation.9 | convolution fusion | flops 4860936192 | bytes 13410304 | tf_op jit(solution)/shard_map/dot_general | solution.py:62
  455.0 9.2 %convolution_convert_fusion.5 = bf16[1024,1024]{1,0:T(8,128)(2,1)} fusion(bf16[1024,2304]{1,0:T(8,128)(2,1)} %all-gather.9.cloned.1.call-done, bf16[1024,16]{1,0:T(8,128)(2,1)S(1)} %bitcast.289, bf16[1024,128]{1,0:T(8,128)(2,1)S(1)} %bitcast.284, bf16[1024,1024]{1,0:T(8,128)(2,1)} %bitcast.341, bf16[1024,1024]{1,0:T(8,128)(2,1)} %get-tuple-element.100), kind=kOutput, calls=%fused_computation.54 | convolution fusion | flops 4856479744 | bytes 11304960 | tf_op jit(solution)/shard_map/dot_general | solution.py:62
  466.8 2.9 collective-permute-done.29
  469.7 2.0 collective-permute-done.27
  472.2 5.2 multiply_reduce_fusion
  477.4 34.5 %reduce-scatter.5.cloned.1.call-done = bf16[256,2304]{1,0:T(8,128)(2,1)} async-done(((bf16[1024,2304]{1,0:T(8,128)(2,1)}), bf16[256,2304]{1,0:T(8,128)(2,1)}) %reduce-scatter.5.cloned.1.call-update) | async-done | bytes 1179664 | tf_op jit(solution)/shard_map/reduce_scatter | solution.py:485
  512.1 7.4 fusion.4
  519.7 12.7 %shard_map.268 = (bf16[1024,1024]{1,0:T(8,128)(2,1)S(1)}, bf16[1024,1024]{1,0:T(8,128)(2,1)}, f32[2,1,1024]{2,1,0:T(1,128)S(1)}, bf16[2,1024,128]{2,1,0:T(8,128)(2,1)}) custom-call(bf16[1024,1024]{1,0:T(8,128)(2,1)} %get-tuple-element.233.grad_ref, bf16[1024,1024]{1,0:T(8,128)(2,1)} %all-gather.7.cloned.1.call-done.weight_ref, ...), custom_call_target="tpu_custom_call" | custom-call | tf_op jit(solution)/shard_map/pallas_call | solution.py:404
  537.7 3.8 fusion.25
  541.8 9.8 %collective-permute-done.30 = bf16[2,1024,128]{2,1,0:T(8,128)(2,1)S(1)} collective-permute-done((bf16[2,1024,128]{2,1,0:T(8,128)(2,1)}, bf16[2,1024,128]{2,1,0:T(8,128)(2,1)S(1)}, u32[]{:S(2)}, u32[]{:S(2)}) %collective-permute-start.30) | collective-permute-done | bytes 524320 | tf_op jit(solution)/shard_map/ppermute | solution.py:27
  551.6 10.2 %collective-permute-done.28 = bf16[2,1024,128]{2,1,0:T(8,128)(2,1)S(1)} collective-permute-done((bf16[2,1024,128]{2,1,0:T(8,128)(2,1)}, bf16[2,1024,128]{2,1,0:T(8,128)(2,1)S(1)}, u32[]{:S(2)}, u32[]{:S(2)}) %collective-permute-start.28) | collective-permute-done | bytes 524320 | tf_op jit(solution)/shard_map/ppermute | solution.py:27
  561.8 2.7 multiply_reduce_fusion.3
  565.7 38.7 %shard_map.269 = (bf16[1024,1024]{1,0:T(8,128)(2,1)}, f32[2,8,1024]{2,1,0:T(8,128)S(1)}, f32[2,4,1024]{2,1,0:T(4,128)S(1)}, f32[2,1,1024]{2,1,0:T(1,128)S(1)}, f...) custom-call(bf16[1024,1024]{1,0:T(8,128)(2,1)} %copy-done, ...), custom_call_target="tpu_custom_call" | custom-call | tf_op jit(solution)/shard_map/pallas_call | solution.py:427
  607.0 2.4 fusion.104
  612.8 4.3 collective-permute-done.32
  619.5 10.2 %convolution_convert_fusion = bf16[1024,2304]{1,0:T(8,128)(2,1)} fusion(bf16[1024,1024]{1,0:T(8,128)(2,1)} %copy-done.62, bf16[1024,16]{1,0:T(8,128)(2,1)S(1)} %bitcast.286, bf16[1024,128]{1,0:T(8,128)(2,1)S(1)} %bitcast.281, bf16[1024,1024]{1,0:T(8,128)(2,1)} %bitcast.336, bf16[1024,1024]{1,0:T(8,128)(2,1)} %get-tuple-element.111), kind=kOutput, calls=%fused_computation.8 | convolution fusion | flops 4857790464 | bytes 11304960 | tf_op jit(solution)/shard_map/dot_general | solution.py:62
  630.1 9.3 %convolution_convert_fusion.4 = bf16[1024,1024]{1,0:T(8,128)(2,1)} fusion(bf16[1024,2304]{1,0:T(8,128)(2,1)} %all-gather.5.cloned.1.call-done, bf16[1024,16]{1,0:T(8,128)(2,1)S(1)} %bitcast.287, bf16[1024,128]{1,0:T(8,128)(2,1)S(1)} %bitcast.282, bf16[1024,1024]{1,0:T(8,128)(2,1)} %bitcast.337, bf16[1024,1024]{1,0:T(8,128)(2,1)} %get-tuple-element.111), kind=kOutput, calls=%fused_computation.53 | convolution fusion | flops 4856479744 | bytes 11304960 | tf_op jit(solution)/shard_map/dot_general | solution.py:62
  640.2 3.8 collective-permute-done.33
  644.0 4.9 fusion.12
  649.1 75.3 %psum.35 = f32[15712]{0:T(1024)S(1)} all-reduce(f32[15712]{0:T(1024)S(1)} %concatenate.39), channel_id=1, replica_groups=mesh['dp'=4,'ctx'=4,'tensor'=2] {'dp','ctx'}, use_global_device_ids=true, to_apply=%region_38.39 | all-reduce | flops 15712 | bytes 125696 | tf_op jit(solution)/shard_map/psum | solution.py:510
  729.0 10.6 %fusion.8 = (f32[1024,1024]{1,0:T(8,128)}, f32[1024,1024]{1,0:T(8,128)}) fusion(bf16[2,512,1024]{2,1,0:T(8,128)(2,1)S(1)} %copy-done.51, bf16[1024,1024]{1,0:T(8,128)(2,1)} %collective-permute-done.33, bf16[1024,1024]{1,0:T(8,128)(2,1)} %convolution_convert_fusion.4, f32[1024]{0:T(1024)S(1)} %multiply_multiply_fusion.2, f32[1024]{0:T(1024)S(1)} %bitcast.302, ...), kind=kLoop, calls=%fused_computation.20 | loop fusion | flops 26214400 | bytes 29388800 | tf_op jit(solution)/shard_map/add | solution.py:487
  742.2 56.5 %all-reduce.27.cloned.1.call-done = (bf16[256,2304]{1,0:T(8,128)(2,1)}, bf16[1,1024,256]{1,2,0:T(8,128)(2,1)}) async-done(((bf16[256,2304]{1,0:T(8,128)(2,1)}, bf16[1,1024,256]{1,2,0:T(8,128)(2,1)}), (bf16[256,2304]{1,0:T(8,128)(2,1)}, bf16[1,1024,256]{1,2,0:T(8,128)(2,1)})) %all-reduce.27.cloned.1.call-update) | async-done | bytes 1703952 | tf_op jit(solution)/shard_map/psum | solution.py:488
  804.8 1.8 copy.148
  808.0 5.9 maximum_convert_fusion
  (506 shorter events, 121.2 us)
Async XLA Ops:
  7.2 66.6 %all-gather.5.cloned.1.call-start = ((), (), s32[]{:S(2)}) async-start(), calls=%async_computation.4 | async-start | bytes 5898240 | tf_op jit(solution)/shard_map/all_gather | solution.py:329
  12.7 62.8 %copy-start.126 = (f32[2,128]{1,0:T(2,128)S(1)}, f32[2,128]{1,0:T(2,128)}, u32[]{:S(2)}) copy-start(f32[2,128]{1,0:T(2,128)} %param.28) | copy-start | bytes 3076
  12.7 63.3 %copy-start.127 = (f32[2,16]{1,0:T(2,128)S(1)}, f32[2,16]{1,0:T(2,128)}, u32[]{:S(2)}) copy-start(f32[2,16]{1,0:T(2,128)} %param.29) | copy-start | bytes 388
  12.7 63.8 %copy-start.111 = (f32[2,4,128]{2,1,0:T(4,128)S(1)}, f32[2,4,128]{2,1,0:T(4,128)}, u32[]{:S(2)}) copy-start(f32[2,4,128]{2,1,0:T(4,128)} %param.27) | copy-start | bytes 12292
  12.7 64.4 %copy-start.50 = (bf16[2,512,1024]{2,1,0:T(8,128)(2,1)S(1)}, bf16[2,512,1024]{2,1,0:T(8,128)(2,1)}, u32[]{:S(2)}) copy-start(bf16[2,512,1024]{2,1,0:T(8,128)(2,1)} %param.19) | copy-start | bytes 6291460
  13.9 63.8 %copy-start.92 = (f32[2,1024]{1,0:T(2,128)S(1)}, f32[2,1024]{1,0:T(2,128)}, u32[]{:S(2)}) copy-start(f32[2,1024]{1,0:T(2,128)} %param.21) | copy-start | bytes 24580
  13.9 63.8 %copy-start.93 = (f32[2,1024]{1,0:T(2,128)S(1)}, f32[2,1024]{1,0:T(2,128)}, u32[]{:S(2)}) copy-start(f32[2,1024]{1,0:T(2,128)} %param.26) | copy-start | bytes 24580
  13.9 63.8 %copy-start.90 = (f32[2,4,1024]{2,1,0:T(4,128)S(1)}, f32[2,4,1024]{2,1,0:T(4,128)}, u32[]{:S(2)}) copy-start(f32[2,4,1024]{2,1,0:T(4,128)} %param.25) | copy-start | bytes 98308
  13.9 163.2 %all-gather.7.cloned.1.call-start = ((), (), s32[]{:S(2)}) async-start(), calls=%async_computation.5 | async-start | bytes 2621440 | tf_op jit(solution)/shard_map/all_gather | solution.py:329
  73.8 119.9 %all-gather.9.cloned.1.call-start = ((), (), s32[]{:S(2)}) async-start(), calls=%async_computation.6 | async-start | bytes 5898240 | tf_op jit(solution)/shard_map/all_gather | solution.py:329
  77.7 116.1 %copy-start.72 = (f32[1,1024]{1,0:T(1,128)}, f32[1,1024]{1,0:T(1,128)S(1)}, u32[]{:S(2)}) copy-start(f32[1,1024]{1,0:T(1,128)S(1)} %get-tuple-element.294) | copy-start | bytes 12292
  77.7 136.0 %copy-start.39 = (f32[1,1024]{1,0:T(1,128)}, f32[1,1024]{1,0:T(1,128)S(1)}, u32[]{:S(2)}) copy-start(f32[1,1024]{1,0:T(1,128)S(1)} %get-tuple-element.292.bias_ref) | copy-start | bytes 12292
  77.8 136.0 %copy-start.27 = (f32[4,1024]{1,0:T(4,128)}, f32[4,1024]{1,0:T(4,128)S(1)}, u32[]{:S(2)}) copy-start(f32[4,1024]{1,0:T(4,128)S(1)} %get-tuple-element.286.taps_ref) | copy-start | bytes 49156
  79.0 207.3 %all-gather.11.cloned.1.call-start = ((), (), s32[]{:S(2)}) async-start(), calls=%async_computation.7 | async-start | bytes 2621440 | tf_op jit(solution)/shard_map/all_gather | solution.py:329
  79.1 130.2 %copy-start.119 = (f32[16]{0:T(128)}, f32[16]{0:T(128)S(1)}, u32[]{:S(2)}) copy-start(f32[16]{0:T(128)S(1)} %get-tuple-element.318) | copy-start | bytes 196
  92.2 5.6 collective-permute-start
  98.9 2.7 collective-permute-start.1
  101.7 56.1 %copy-start.5 = (bf16[1024,128]{1,0:T(8,128)(2,1)}, bf16[1024,128]{1,0:T(8,128)(2,1)S(1)}, u32[]{:S(2)}) copy-start(bf16[1024,128]{1,0:T(8,128)(2,1)S(1)} %get-tuple-element.265.keys_ref) | copy-start | bytes 786436
  116.3 39.7 %collective-permute-start.6 = (bf16[2,1024,128]{2,1,0:T(8,128)(2,1)S(1)}, bf16[2,1024,128]{2,1,0:T(8,128)(2,1)S(1)}, u32[]{:S(2)}, u32[]{:S(2)}) collective-permute-start(bf16[2,1024,128]{2,1,0:T(8,128)(2,1)S(1)} %get-tuple-element.88), channel_id=1, source_target_pairs={{0,6},{1,7},{8,14},{9,15},{16,22},{17,23},{24,30},{25,31}} | collective-permute-start | bytes 1572872 | tf_op jit(solution)/shard_map/ppermute | solution.py:27
  119.6 36.4 %collective-permute-start.4 = (bf16[2,1024,128]{2,1,0:T(8,128)(2,1)S(1)}, bf16[2,1024,128]{2,1,0:T(8,128)(2,1)S(1)}, u32[]{:S(2)}, u32[]{:S(2)}) collective-permute-start(bf16[2,1024,128]{2,1,0:T(8,128)(2,1)S(1)} %get-tuple-element.88), channel_id=1, source_target_pairs={{0,4},{2,6},{1,5},{3,7},{8,12},{10,14},{9,13},{11,15},{16,20},{18,... | collective-permute-start | bytes 1572872 | tf_op jit(solution)/shard_map/ppermute | solution.py:27
  121.4 34.7 %collective-permute-start.2 = (bf16[2,1024,128]{2,1,0:T(8,128)(2,1)S(1)}, bf16[2,1024,128]{2,1,0:T(8,128)(2,1)}, u32[]{:S(2)}, u32[]{:S(2)}) collective-permute-start(bf16[2,1024,128]{2,1,0:T(8,128)(2,1)S(1)} %get-tuple-element.88), channel_id=1, source_target_pairs={{0,2},{2,4},{4,6},{1,3},{3,5},{5,7},{8,10},{10,12},{12,14},{9,11},... | collective-permute-start | bytes 1572872 | tf_op jit(solution)/shard_map/ppermute | solution.py:27
  124.4 51.4 %copy-start.29 = (f32[1,1024]{1,0:T(1,128)}, f32[1,1024]{1,0:T(1,128)S(1)}, u32[]{:S(2)}) copy-start(f32[1,1024]{1,0:T(1,128)S(1)} %broadcast_in_dim_reshape.4.skip_ref) | copy-start | bytes 12292
  125.0 50.8 %copy-start.33 = (f32[1,1024]{1,0:T(1,128)}, f32[1,1024]{1,0:T(1,128)S(1)}, u32[]{:S(2)}) copy-start(f32[1,1024]{1,0:T(1,128)S(1)} %get-tuple-element.291.gain_ref) | copy-start | bytes 12292
  125.0 50.8 %copy-start.129 = (f32[2,1,16]{2,1,0:T(1,128)}, f32[2,1,16]{2,1,0:T(1,128)S(1)}, u32[]{:S(2)}) copy-start(f32[2,1,16]{2,1,0:T(1,128)S(1)} %slice.429) | copy-start | bytes 388
  125.0 30.7 %collective-permute-start.5 = (f32[2,16]{1,0:T(2,128)S(1)}, f32[2,16]{1,0:T(2,128)S(1)}, u32[]{:S(2)}, u32[]{:S(2)}) collective-permute-start(f32[2,16]{1,0:T(2,128)S(1)} %bitcast.326), channel_id=1, source_target_pairs={{0,4},{2,6},{1,5},{3,7},{8,12},{10,14},{9,13},{11,15},{16,20},{18,... | collective-permute-start | bytes 392 | tf_op jit(solution)/shard_map/ppermute | solution.py:27
  126.3 29.5 %collective-permute-start.3 = (f32[2,16]{1,0:T(2,128)S(1)}, f32[2,16]{1,0:T(2,128)S(1)}, u32[]{:S(2)}, u32[]{:S(2)}) collective-permute-start(f32[2,16]{1,0:T(2,128)S(1)} %bitcast.327), channel_id=1, source_target_pairs={{0,2},{2,4},{4,6},{1,3},{3,5},{5,7},{8,10},{10,12},{12,14},{9,11},... | collective-permute-start | bytes 392 | tf_op jit(solution)/shard_map/ppermute | solution.py:27
  183.1 4.5 collective-permute-start.7
  183.3 3.8 collective-permute-start.8
  193.7 283.7 %reduce-scatter.7.cloned.1.call-start = ((), (), s32[]{:S(2)}) async-start(), calls=%async_computation.9 | async-start | bytes 2621440 | tf_op jit(solution)/shard_map/reduce_scatter | solution.py:426
  202.4 5.7 collective-permute-start.9
  209.3 2.7 collective-permute-start.10
  213.8 47.3 %copy-start.7 = (bf16[1024,128]{1,0:T(8,128)(2,1)}, bf16[1024,128]{1,0:T(8,128)(2,1)S(1)}, u32[]{:S(2)}) copy-start(bf16[1024,128]{1,0:T(8,128)(2,1)S(1)} %get-tuple-element.263.keys_ref) | copy-start | bytes 786436
  229.1 32.0 %collective-permute-start.15 = (bf16[2,1024,128]{2,1,0:T(8,128)(2,1)}, bf16[2,1024,128]{2,1,0:T(8,128)(2,1)}, u32[]{:S(2)}, u32[]{:S(2)}) collective-permute-start(bf16[2,1024,128]{2,1,0:T(8,128)(2,1)} %get-tuple-element.95), channel_id=1, source_target_pairs={{0,6},{1,7},{8,14},{9,15},{16,22},{17,23},{24,30},{25,31}} | collective-permute-start | bytes 1572872 | tf_op jit(solution)/shard_map/ppermute | solution.py:27
  234.0 27.1 %collective-permute-start.13 = (bf16[2,1024,128]{2,1,0:T(8,128)(2,1)}, bf16[2,1024,128]{2,1,0:T(8,128)(2,1)}, u32[]{:S(2)}, u32[]{:S(2)}) collective-permute-start(bf16[2,1024,128]{2,1,0:T(8,128)(2,1)} %get-tuple-element.95), channel_id=1, source_target_pairs={{0,4},{2,6},{1,5},{3,7},{8,12},{10,14},{9,13},{11,15},{16,20},{18,... | collective-permute-start | bytes 1572872 | tf_op jit(solution)/shard_map/ppermute | solution.py:27
  236.9 24.2 %collective-permute-start.11 = (bf16[2,1024,128]{2,1,0:T(8,128)(2,1)}, bf16[2,1024,128]{2,1,0:T(8,128)(2,1)}, u32[]{:S(2)}, u32[]{:S(2)}) collective-permute-start(bf16[2,1024,128]{2,1,0:T(8,128)(2,1)} %get-tuple-element.95), channel_id=1, source_target_pairs={{0,2},{2,4},{4,6},{1,3},{3,5},{5,7},{8,10},{10,12},{12,14},{9,11},... | collective-permute-start | bytes 1572872 | tf_op jit(solution)/shard_map/ppermute | solution.py:27
  239.8 19.8 %collective-permute-start.14 = (f32[2,16]{1,0:T(2,128)S(1)}, f32[2,16]{1,0:T(2,128)S(1)}, u32[]{:S(2)}, u32[]{:S(2)}) collective-permute-start(f32[2,16]{1,0:T(2,128)S(1)} %bitcast.330), channel_id=1, source_target_pairs={{0,4},{2,6},{1,5},{3,7},{8,12},{10,14},{9,13},{11,15},{16,20},{18,... | collective-permute-start | bytes 392 | tf_op jit(solution)/shard_map/ppermute | solution.py:27
  241.1 18.5 %collective-permute-start.12 = (f32[2,16]{1,0:T(2,128)S(1)}, f32[2,16]{1,0:T(2,128)S(1)}, u32[]{:S(2)}, u32[]{:S(2)}) collective-permute-start(f32[2,16]{1,0:T(2,128)S(1)} %bitcast.331), channel_id=1, source_target_pairs={{0,2},{2,4},{4,6},{1,3},{3,5},{5,7},{8,10},{10,12},{12,14},{9,11},... | collective-permute-start | bytes 392 | tf_op jit(solution)/shard_map/ppermute | solution.py:27
  292.3 14.0 %collective-permute-start.16 = (bf16[1024,1024]{1,0:T(8,128)(2,1)}, bf16[1024,1024]{1,0:T(8,128)(2,1)}, u32[]{:S(2)}, u32[]{:S(2)}) collective-permute-start(bf16[1024,1024]{1,0:T(8,128)(2,1)} %convolution_convert_fusion.6), channel_id=1, source_target_pairs={{0,1},{1,0},{2,3},{3,2},{4,5},{5,4},{6,7},{7,6},{8,9},{9,8},{10,11... | collective-permute-start | bytes 6291464 | tf_op jit(solution)/shard_map/ppermute | solution.py:31
  292.3 5.5 collective-permute-start.21
  293.6 5.5 collective-permute-start.19
  306.3 3.8 collective-permute-start.17
  332.4 17.9 %collective-permute-start.22 = (bf16[2,1024,128]{2,1,0:T(8,128)(2,1)}, bf16[2,1024,128]{2,1,0:T(8,128)(2,1)}, u32[]{:S(2)}, u32[]{:S(2)}) collective-permute-start(bf16[2,1024,128]{2,1,0:T(8,128)(2,1)} %get-tuple-element.101), channel_id=1, source_target_pairs={{6,0},{7,1},{14,8},{15,9},{22,16},{23,17},{30,24},{31,25}} | collective-permute-start | bytes 1572872 | tf_op jit(solution)/shard_map/ppermute | solution.py:27
  333.7 34.5 %collective-permute-start.20 = (bf16[2,1024,128]{2,1,0:T(8,128)(2,1)}, bf16[2,1024,128]{2,1,0:T(8,128)(2,1)}, u32[]{:S(2)}, u32[]{:S(2)}) collective-permute-start(bf16[2,1024,128]{2,1,0:T(8,128)(2,1)} %get-tuple-element.101), channel_id=1, source_target_pairs={{4,0},{6,2},{5,1},{7,3},{12,8},{14,10},{13,9},{15,11},{20,16},{22,... | collective-permute-start | bytes 1572872 | tf_op jit(solution)/shard_map/ppermute | solution.py:27
  335.0 33.2 %collective-permute-start.18 = (bf16[2,1024,128]{2,1,0:T(8,128)(2,1)}, bf16[2,1024,128]{2,1,0:T(8,128)(2,1)}, u32[]{:S(2)}, u32[]{:S(2)}) collective-permute-start(bf16[2,1024,128]{2,1,0:T(8,128)(2,1)} %get-tuple-element.101), channel_id=1, source_target_pairs={{2,0},{4,2},{6,4},{3,1},{5,3},{7,5},{10,8},{12,10},{14,12},{11,9},... | collective-permute-start | bytes 1572872 | tf_op jit(solution)/shard_map/ppermute | solution.py:27
  340.2 171.8 %reduce-scatter.5.cloned.1.call-start = ((), (), s32[]{:S(2)}) async-start(), calls=%async_computation.8 | async-start | bytes 5898240 | tf_op jit(solution)/shard_map/reduce_scatter | solution.py:485
  420.4 6.2 collective-permute-start.23
  429.9 8.2 %collective-permute-start.24 = (f32[2,3,1152]{2,1,0:T(4,128)S(1)}, f32[2,3,1152]{2,1,0:T(4,128)S(1)}, u32[]{:S(2)}, u32[]{:S(2)}) collective-permute-start(f32[2,3,1152]{2,1,0:T(4,128)S(1)} %pad_maximum_fusion.2), channel_id=1, source_target_pairs={{2,0},{4,2},{6,4},{3,1},{5,3},{7,5},{10,8},{12,10},{14,12},{11,9},... | collective-permute-start | bytes 82952 | tf_op jit(solution)/shard_map/ppermute | solution.py:27
  454.0 165.5 %all-reduce.29.cloned.1.call-start = ((), (), s32[]{:S(2)}) async-start(), calls=%async_computation.13 | async-start | bytes 3407872 | tf_op jit(solution)/shard_map/psum | solution.py:488
  464.2 8.0 collective-permute-start.25
  464.2 5.5 collective-permute-start.29
  465.5 6.2 collective-permute-start.27
  512.0 216.9 %reduce-scatter.11.cloned.1.call-start = ((), (), s32[]{:S(2)}) async-start(), calls=%async_computation.11 | async-start | bytes 2621440 | tf_op jit(solution)/shard_map/reduce_scatter | solution.py:426
  533.8 17.8 %collective-permute-start.30 = (bf16[2,1024,128]{2,1,0:T(8,128)(2,1)}, bf16[2,1024,128]{2,1,0:T(8,128)(2,1)S(1)}, u32[]{:S(2)}, u32[]{:S(2)}) collective-permute-start(bf16[2,1024,128]{2,1,0:T(8,128)(2,1)} %get-tuple-element.112), channel_id=1, source_target_pairs={{6,0},{7,1},{14,8},{15,9},{22,16},{23,17},{30,24},{31,25}} | collective-permute-start | bytes 1572872 | tf_op jit(solution)/shard_map/ppermute | solution.py:27
  535.1 26.8 %collective-permute-start.28 = (bf16[2,1024,128]{2,1,0:T(8,128)(2,1)}, bf16[2,1024,128]{2,1,0:T(8,128)(2,1)S(1)}, u32[]{:S(2)}, u32[]{:S(2)}) collective-permute-start(bf16[2,1024,128]{2,1,0:T(8,128)(2,1)} %get-tuple-element.112), channel_id=1, source_target_pairs={{4,0},{6,2},{5,1},{7,3},{12,8},{14,10},{13,9},{15,11},{20,16},{22,... | collective-permute-start | bytes 1572872 | tf_op jit(solution)/shard_map/ppermute | solution.py:27
  536.4 25.5 %collective-permute-start.26 = (bf16[2,1024,128]{2,1,0:T(8,128)(2,1)}, bf16[2,1024,128]{2,1,0:T(8,128)(2,1)}, u32[]{:S(2)}, u32[]{:S(2)}) collective-permute-start(bf16[2,1024,128]{2,1,0:T(8,128)(2,1)} %get-tuple-element.112), channel_id=1, source_target_pairs={{2,0},{4,2},{6,4},{3,1},{5,3},{7,5},{10,8},{12,10},{14,12},{11,9},... | collective-permute-start | bytes 1572872 | tf_op jit(solution)/shard_map/ppermute | solution.py:27
  541.5 187.4 %reduce-scatter.9.cloned.1.call-start = ((), (), s32[]{:S(2)}) async-start(), calls=%async_computation.10 | async-start | bytes 5898240 | tf_op jit(solution)/shard_map/reduce_scatter | solution.py:485
  565.7 41.3 %copy-start.120 = (f32[16]{0:T(128)S(1)}, f32[16]{0:T(128)}, u32[]{:S(2)}) copy-start(f32[16]{0:T(128)} %get-tuple-element.304) | copy-start | bytes 196
  604.6 4.8 collective-permute-start.31
  611.1 6.0 collective-permute-start.32
  629.8 168.9 %all-reduce.27.cloned.1.call-start = ((), (), s32[]{:S(2)}) async-start(), calls=%async_computation.12 | async-start | bytes 3407872 | tf_op jit(solution)/shard_map/psum | solution.py:488
  639.4 89.5 %copy-start.89 = (f32[1,4,2,128]{3,1,2,0:T(4,128)S(1)}, f32[1,4,2,128]{3,1,2,0:T(4,128)}, u32[]{:S(2)}) copy-start(f32[1,4,2,128]{3,1,2,0:T(4,128)} %copy-done.88) | copy-start | bytes 12292
  639.4 4.6 collective-permute-start.33
  640.2 88.8 %copy-start.51 = (bf16[2,512,1024]{2,1,0:T(8,128)(2,1)S(1)}, bf16[2,512,1024]{2,1,0:T(8,128)(2,1)}, u32[]{:S(2)}) copy-start(bf16[2,512,1024]{2,1,0:T(8,128)(2,1)} %param.19) | copy-start | bytes 6291460
  640.2 88.8 %copy-start.81 = (f32[1024]{0:T(1024)S(1)}, f32[1024]{0:T(1024)}, u32[]{:S(2)}) copy-start(f32[1024]{0:T(1024)} %get-tuple-element.235) | copy-start | bytes 12292
  (115 other events, 1157.4 us)
Sparse Core Ops, SparseCore 0:
  14.0 59.7 all-gather.4
  76.2 35.3 all-gather.6
  113.4 77.9 all-gather.8
  193.8 36.3 all-gather.10
  340.3 48.0 reduce-scatter.6
  454.1 57.8 reduce-scatter.4
  514.6 73.7 all-reduce.28
  592.1 34.2 reduce-scatter.10
  629.9 59.5 reduce-scatter.8
  729.1 69.5 all-reduce.26
